TPU v7x, 256 devices: a whole 4x4x8 slice. The times are simulated.
256 devices in a mesh: tm: 16 (over y_hi, x, core), space: 16 (over y_lo, z).
Axes of the slice: x: 4, y: 4 (y_hi: 2, y_lo: 2; y = y_hi * 2 + y_lo), z: 8, core: 2. Of those that a mesh axis runs over, the one named last changes fastest.
Arguments:
- initial_starts: float32 [16, 1024, 2048], P('tm', None, 'space'), may hold values from -6 to 6
- source: float32 [16, 1024, 2048], P('tm', None, 'space'), may hold values from -12 to 12
- region: int32 [1024, 2048], P(None, 'space'), may hold values from 0 to 7
- base_reluctivity: float32 [8], replicated, may hold values from 0.4 to 1
- saturation: float32 [8], replicated, may hold values from 0.2 to 1
- mobility: float32 [8], replicated, may hold values from 0.01 to 0.12
Outputs:
- final_starts: float32 [16, 1024, 2048], P('tm', None, 'space')
- fine_ends: float32 [16, 1024, 2048], P('tm', None, 'space')
All inputs are finite; a program needn't handle non-finite values.
Results may differ from a plain program's by a relative error of at most 0.00002.
Values sent between devices are 32-bit elements; how exact they have to be, the bound alone decides.
A program may use at most 64 MiB of HBM per device.

v0:
```python
import jax
import jax.numpy as jnp
from jax import lax
from jax.experimental import pallas as pl
from jax.experimental.pallas import tpu as pltpu
from jax.sharding import PartitionSpec as P

MESH = pl.DeviceIdType.MESH
HALO = 6
HALF = 64
FRAME = HALF + 2 * HALO
OWN = HALF + HALO
ROWS = 8
F32 = jnp.float32


def rows(col, n):
    start = col * ROWS
    if not isinstance(start, int):
        start = pl.multiple_of(start, ROWS)
    return pl.ds(start, n * ROWS)


def kernel(
    base_ref, satur_ref, mob_ref, a_hbm, j_hbm, r_hbm, starts_hbm, ends_hbm,
    in_a, in_j, in_r, ta, tj, tr, starts, drive, regions, coef_a, coef_b, mobile, gain,
    work, ends, corr0, items, got, sums, out_e, out_s,
    in_sem, pair_send, pair_recv, edge_send, edge_recv, reg_send, reg_recv,
    there_send, there_recv, back_send, back_recv, halo_send, halo_recv, out_send, out_recv, out_sem,
):
    tm = lax.axis_index("tm")
    sp = lax.axis_index("space")
    core = lax.rem(tm, 2)
    other = 1 - core
    pair = tm - core
    chip = tm // 2
    right = lax.rem(sp + 1, 16)
    left = lax.rem(sp + 15, 16)
    outer = jnp.where(core == 0, left, right)
    ahead = jnp.where(core == 0, right, left)

    loads = []
    for n, (src, dst) in enumerate(((a_hbm, in_a), (r_hbm, in_r), (j_hbm, in_j))):
        cp = pltpu.make_async_copy(src, dst, in_sem.at[n])
        cp.start()
        loads.append(cp)

    barrier = pltpu.get_barrier_semaphore()
    pl.semaphore_signal(barrier, inc=1, device_id=(pair + other, sp), device_id_type=MESH)
    for d in range(1, 8):
        pl.semaphore_signal(
            barrier, inc=1, device_id=(2 * lax.rem(chip + d, 8) + core, sp), device_id_type=MESH
        )
    pl.semaphore_signal(barrier, inc=1, device_id=(pair, outer), device_id_type=MESH)
    pl.semaphore_signal(barrier, inc=1, device_id=(pair + 1, outer), device_id_type=MESH)

    def turn(src, dst):
        for s in range(8):
            dst[pl.ds(s, 128, stride=8), :] = src[pl.ds(128 * s, 128), :].T

    loads[0].wait()
    turn(in_a.at[0], ta)
    loads[1].wait()
    turn(in_r, tr)
    loads[2].wait()
    turn(in_j.at[0], tj)

    pl.semaphore_wait(barrier, 10)

    sends = []
    for n, (src, dst) in enumerate(((ta, starts.at[0]), (tj, drive))):
        cp = pltpu.make_async_remote_copy(
            src.at[rows(122, 6)], dst.at[core, rows(0, 6)],
            edge_send.at[n, 0], edge_recv.at[n, core], device_id=(pair, right), device_id_type=MESH,
        )
        cp.start()
        sends.append(cp)
        cp = pltpu.make_async_remote_copy(
            src.at[rows(0, 6)], dst.at[core, rows(OWN, 6)],
            edge_send.at[n, 1], edge_recv.at[n, core], device_id=(pair + 1, left), device_id_type=MESH,
        )
        cp.start()
        sends.append(cp)
    cp_reg = pltpu.make_async_remote_copy(
        tr.at[rows(122 * other, 6)], regions.at[rows(OWN * core, 6)],
        reg_send, reg_recv, device_id=(tm, ahead), device_id_type=MESH,
    )
    cp_reg.start()
    sends.append(cp_reg)
    pairs = []
    for n, (src, dst) in enumerate(((ta, starts.at[0]), (tj, drive))):
        cp = pltpu.make_async_remote_copy(
            src.at[rows(58 * other, OWN)], dst.at[core, rows(HALO * core, OWN)],
            pair_send.at[n], pair_recv.at[n], device_id=(pair + other, sp), device_id_type=MESH,
        )
        cp.start()
        pairs.append(cp)

    starts[0, core, rows(HALO * other, OWN), :] = ta[rows(58 * core, OWN), :]
    drive[core, rows(HALO * other, OWN), :] = tj[rows(58 * core, OWN), :]
    regions[rows(HALO * other, OWN), :] = tr[rows(58 * core, OWN), :]

    cp_reg.wait_recv()
    full = lambda x: jnp.full((8, 128), x, F32)
    base = [full(base_ref[k]) for k in range(8)]
    satur = [full(satur_ref[k]) for k in range(8)]
    mobs = [full(mob_ref[k]) for k in range(8)]
    tab_a = [0.5 * b * (1.0 + s) for b, s in zip(base, satur)]
    tab_b = [2.0 * b * s for b, s in zip(base, satur)]
    tab_c = [1.0 / (1.0 + 12.0 * m * b) for b, m in zip(base, mobs)]

    def lookup(t, _):
        r = regions[rows(t, 1), :]
        bits = [(r & 1) != 0, (r & 2) != 0, (r & 4) != 0]
        for tab, ref in ((tab_a, coef_a), (tab_b, coef_b), (mobs, mobile), (tab_c, gain)):
            level = tab
            for bit in bits:
                level = [jnp.where(bit, hi, lo) for lo, hi in zip(level[::2], level[1::2])]
            ref[rows(t, 1), :] = level[0]
        return 0

    lax.fori_loop(0, FRAME, lookup, 0)

    lane = lax.broadcasted_iota(jnp.int32, (8, 128), 1)
    sub = lax.broadcasted_iota(jnp.int32, (8, 128), 0)
    last_lane = lane == 127
    first_lane = lane == 0
    top = last_lane & (sub == 7)
    bottom = first_lane & (sub == 0)

    def up(x, end):
        r = pltpu.roll(x, 127, 1)
        return jnp.where(top, end, jnp.where(last_lane, pltpu.roll(r, 7, 0), r))

    def down(x, end):
        r = pltpu.roll(x, 1, 1)
        return jnp.where(bottom, end, jnp.where(first_lane, pltpu.roll(r, 1, 0), r))

    def fine(src, dst, lo, hi, shift):
        def column(before, here, after, t):
            north = up(here, 0.0)
            south = down(here, 0.0)
            br = north - south
            bt = after - before
            nu = coef_a[rows(t, 1), :] - coef_b[rows(t, 1), :] / (4.0 + (br * br + bt * bt))
            nu_n = up(nu, nu)
            nu_s = down(nu, nu)
            radial = (nu + nu_n) * (north - here) + (nu + nu_s) * (south - here)
            return nu, radial

        first = []
        for p in range(2):
            a = [src[p, rows(lo - 2 + k, 1), :] for k in range(4)]
            nu_w, _ = column(a[0], a[1], a[2], lo - 1)
            nu, radial = column(a[1], a[2], a[3], lo)
            west = (nu_w + nu) * (a[2] - a[1])
            first.append((a[2], a[3], nu, radial, west))

        def body(t, carry):
            out = []
            for p in range(2):
                here, after, nu, radial, west = carry[p]
                beyond = src[p, rows(t + 2, 1), :]
                nu_e, radial_e = column(here, after, beyond, t + 1)
                east = (nu + nu_e) * (after - here)
                total = (east - west) + radial + drive[p, rows(t, 1), :]
                dst[p, rows(t - shift, 1), :] = here + mobile[rows(t, 1), :] * total
                out.append((after, beyond, nu_e, radial_e, east))
            return tuple(out)

        def four(i, carry):
            for k in range(4):
                carry = body(lo + 4 * i + k, carry)
            return carry

        lax.fori_loop(0, (hi - lo) // 4, four, tuple(first))

    for cp in pairs:
        cp.wait_recv()
    for n in range(2):
        for p in range(2):
            pltpu.make_async_remote_copy(
                ta.at[rows(0, 6)], starts.at[0, 0, rows(0, 6)],
                edge_send.at[n, 0], edge_recv.at[n, p], device_id=(tm, right), device_id_type=MESH,
            ).wait_recv()

    for it in range(2):
        fine(starts.at[it], work, 2, FRAME - 2, 0)
        fine(work, work, 4, FRAME - 4, 0)
        fine(work, ends.at[it], 6, FRAME - 6, HALO)

        if it == 1:
            cp_e = pltpu.make_async_remote_copy(
                ends.at[1, other], out_e.at[rows(HALF * core, HALF)],
                out_send.at[0], out_recv.at[0], device_id=(pair + other, sp), device_id_type=MESH,
            )
            cp_e.start()
            sends.append(cp_e)

        def combine(t, _):
            c = gain[rows(t + HALO, 1), :]
            e0, e1 = ends[it, 0, rows(t, 1), :], ends[it, 1, rows(t, 1), :]
            k0 = e0 - c * starts[it, 0, rows(t + HALO, 1), :]
            k1 = e1 - c * starts[it, 1, rows(t + HALO, 1), :]
            corr0[rows(t, 1), :] = k0
            items[it, rows(t, 1), :] = jnp.where(chip == 7, e1, c * k0 + k1)
            return 0

        lax.fori_loop(0, HALF, combine, 0)

        there = []
        for d in range(1, 8):
            q = lax.rem(chip + d, 8)
            cp = pltpu.make_async_remote_copy(
                items.at[it, rows(8 * q, 8)], got.at[it, chip],
                there_send.at[it, d], there_recv.at[it, d], device_id=(2 * q + core, sp), device_id_type=MESH,
            )
            cp.start()
            there.append(cp)
        got[it, chip] = items[it, rows(8 * chip, 8), :]
        if it == 1:
            out_e[rows(HALF * core, HALF), :] = ends[1, core]
        for cp in there:
            cp.wait_recv()
        sends += there

        def recur(t, _):
            c = gain[rows(8 * chip + t + HALO, 1), :]
            c2 = c * c
            total = got[it, 7, rows(t, 1), :]
            sums[it, 0, rows(t, 1), :] = total
            for k in range(7):
                total = c2 * total + got[it, k, rows(t, 1), :]
                sums[it, k + 1, rows(t, 1), :] = total
            return 0

        lax.fori_loop(0, 8, recur, 0)

        back = []
        for d in range(1, 8):
            q = lax.rem(chip + d, 8)
            cp = pltpu.make_async_remote_copy(
                sums.at[it, q], starts.at[it + 1, 0, rows(8 * chip + HALO, 8)],
                back_send.at[it, d], back_recv.at[it, d], device_id=(2 * q + core, sp), device_id_type=MESH,
            )
            cp.start()
            back.append(cp)
        starts[it + 1, 0, rows(8 * chip + HALO, 8), :] = sums[it, chip]
        if it == 1:
            cp_e.wait_recv()
            for s in range(8):
                in_a[0, pl.ds(128 * s, 128), :] = out_e[pl.ds(s, 128, stride=8), :].T
            store_e = pltpu.make_async_copy(in_a, ends_hbm, out_sem.at[0])
            store_e.start()
        for cp in back:
            cp.wait_recv()
        sends += back

        def spread(t, _):
            c = gain[rows(t + HALO, 1), :]
            starts[it + 1, 1, rows(t + HALO, 1), :] = (
                c * starts[it + 1, 0, rows(t + HALO, 1), :] + corr0[rows(t, 1), :]
            )
            return 0

        lax.fori_loop(0, HALF, spread, 0)

        if it == 0:
            halos = []
            for n in range(2):
                if n == 0:
                    target = (jnp.where(core == 0, pair + 1, pair), jnp.where(core == 0, left, sp))
                    src, dst = rows(HALO, 6), rows(OWN, 6)
                else:
                    target = (jnp.where(core == 0, pair + 1, pair), jnp.where(core == 0, sp, right))
                    src, dst = rows(HALF, 6), rows(0, 6)
                cp = pltpu.make_async_remote_copy(
                    starts.at[1, :, src], starts.at[1, :, dst],
                    halo_send.at[n], halo_recv.at[n], device_id=target, device_id_type=MESH,
                )
                cp.start()
                halos.append(cp)
            for cp in halos:
                cp.wait_recv()
            sends += halos

    cp_s = pltpu.make_async_remote_copy(
        starts.at[2, other, rows(HALO, HALF)], out_s.at[rows(HALF * core, HALF)],
        out_send.at[1], out_recv.at[1], device_id=(pair + other, sp), device_id_type=MESH,
    )
    cp_s.start()
    sends.append(cp_s)
    out_s[rows(HALF * core, HALF), :] = starts[2, core, rows(HALO, HALF), :]
    cp_s.wait_recv()
    for s in range(8):
        in_j[0, pl.ds(128 * s, 128), :] = out_s[pl.ds(s, 128, stride=8), :].T
    store_s = pltpu.make_async_copy(in_j, starts_hbm, out_sem.at[1])
    store_s.start()
    for cp in sends + pairs:
        cp.wait_send()
    store_e.wait()
    store_s.wait()


def local(initial_starts, source, region, base_reluctivity, saturation, mobility):
    block = jax.ShapeDtypeStruct((1, 1024, 128), F32)
    smem = pl.BlockSpec(memory_space=pltpu.SMEM)
    hbm = pl.BlockSpec(memory_space=pl.ANY)
    big = lambda *lead: pltpu.VMEM(lead + (1024, 128), F32)
    frame = lambda *lead: pltpu.VMEM(lead + (FRAME * ROWS, 128), F32)
    half = lambda *lead: pltpu.VMEM(lead + (HALF * ROWS, 128), F32)
    sem = lambda *shape: pltpu.SemaphoreType.DMA(shape)
    return pl.pallas_call(
        kernel,
        out_shape=(block, block),
        in_specs=[smem] * 3 + [hbm] * 3,
        out_specs=(hbm, hbm),
        scratch_shapes=[
            big(1), big(1), pltpu.VMEM((1024, 128), jnp.int32), big(), big(), pltpu.VMEM((1024, 128), jnp.int32),
            frame(3, 2), frame(2), pltpu.VMEM((FRAME * ROWS, 128), jnp.int32),
            frame(), frame(), frame(), frame(),
            frame(2), half(2, 2), half(), half(2), pltpu.VMEM((2, 8, 64, 128), F32), pltpu.VMEM((2, 8, 64, 128), F32),
            big(), big(),
            sem(3), sem(2), sem(2), sem(2, 2), sem(2, 2), pltpu.SemaphoreType.DMA, pltpu.SemaphoreType.DMA,
            sem(2, 8), sem(2, 8), sem(2, 8), sem(2, 8), sem(2), sem(2), sem(2), sem(2), sem(2),
        ],
        compiler_params=pltpu.CompilerParams(
            collective_id=0, has_side_effects=True, vmem_limit_bytes=40 * 2**20
        ),
        name="parareal",
    )(base_reluctivity, saturation, mobility, initial_starts, source, region)


def solution(mesh):
    in_specs = (P("tm", None, "space"), P("tm", None, "space"), P(None, "space"), P(), P(), P())
    out_specs = (P("tm", None, "space"), P("tm", None, "space"))
    return jax.shard_map(local, mesh=mesh, in_specs=in_specs, out_specs=out_specs, check_vma=False)
```

profile of v0, /device:TPU:1, one launch (start us, length us, event | category | flops | bytes accessed | tf_op | source)
XLA Modules:
  0.0 72.3 jit_solution(194759439083507616)
XLA Ops:
  0.6 0.0 copy-start
  0.6 1.0 %copy-done = f32[1,1024,128]{2,1,0:T(8,128)S(1)} copy-done((f32[1,1024,128]{2,1,0:T(8,128)S(1)}, f32[1,1024,128]{2,1,0:T(8,128)}, u32[]{:S(2)}) %copy-start) | copy-done | bytes 524312
  1.7 0.0 copy-start.1
  1.7 1.0 %copy-done.1 = f32[1,1024,128]{2,1,0:T(8,128)S(1)} copy-done((f32[1,1024,128]{2,1,0:T(8,128)S(1)}, f32[1,1024,128]{2,1,0:T(8,128)}, u32[]{:S(2)}) %copy-start.1) | copy-done | bytes 524312
  2.7 0.0 copy-start.2
  2.7 1.0 %copy-done.2 = s32[1024,128]{1,0:T(8,128)S(1)} copy-done((s32[1024,128]{1,0:T(8,128)S(1)}, s32[1024,128]{1,0:T(8,128)}, u32[]{:S(2)}) %copy-start.2) | copy-done | bytes 524312
  3.8 0.0 copy-start.3
  3.8 0.7 copy-done.3
  4.4 0.0 copy-start.4
  4.4 0.7 copy-done.4
  5.1 0.0 copy-start.5
  5.1 0.7 copy-done.5
  5.7 65.0 %parareal.1 = (f32[1,1024,128]{2,1,0:T(8,128)S(1)}, f32[1,1024,128]{2,1,0:T(8,128)S(1)}) custom-call(f32[8]{0:T(128)S(1)} %copy-done.3, f32[8]{0:T(128)S(1)} %copy-done.4, f32[8]{0:T(128)S(1)} %copy-done.5, f32[1,1024,128]{2,1,0:T(8,128)S(1)} %copy-done, f32[1,1024,128]{2,1,0:T(8,128)S(1)} %copy-done.1, s32[1024,128]{1,0:T(8,128)S(1)} %copy-done.2), custom_call_target="tpu_custom_call" | custom-call | tf_op jit(solution)/shard_map/parareal/pallas_call | solution.py:313
  70.7 0.8 %copy.10 = f32[1,1024,128]{2,1,0:T(8,128)} copy(f32[1,1024,128]{2,1,0:T(8,128)S(1)} %get-tuple-element.4) | data formatting | bytes 1048576
  71.5 0.8 %copy.11 = f32[1,1024,128]{2,1,0:T(8,128)} copy(f32[1,1024,128]{2,1,0:T(8,128)S(1)} %get-tuple-element.5) | data formatting | bytes 1048576
Async XLA Ops:
  0.6 1.0 %copy-start = (f32[1,1024,128]{2,1,0:T(8,128)S(1)}, f32[1,1024,128]{2,1,0:T(8,128)}, u32[]{:S(2)}) copy-start(f32[1,1024,128]{2,1,0:T(8,128)} %a_hbm.1) | copy-start | bytes 1572868
  1.7 1.0 %copy-start.1 = (f32[1,1024,128]{2,1,0:T(8,128)S(1)}, f32[1,1024,128]{2,1,0:T(8,128)}, u32[]{:S(2)}) copy-start(f32[1,1024,128]{2,1,0:T(8,128)} %j_hbm.1) | copy-start | bytes 1572868
  2.7 1.0 %copy-start.2 = (s32[1024,128]{1,0:T(8,128)S(1)}, s32[1024,128]{1,0:T(8,128)}, u32[]{:S(2)}) copy-start(s32[1024,128]{1,0:T(8,128)} %r_hbm.1) | copy-start | bytes 1572868
  3.8 0.7 copy-start.3
  4.4 0.7 copy-start.4
  5.1 0.7 copy-start.5
where the time goes:
time: 72.6 us; the launch traced here: 72.3 us
  Pallas kernels  65 us (90%)
  local copies, waits for them, and re-layouts  6.67 us (9%)
    pallas_call x1, Pallas kernels, local(): pl.pallas_call(kernel, out_shape=(block, block), in_specs=[smem] * 3 + [h...  65 us
    unnamed x14, local copies, waits for them, and re-layouts  6.67 us

commit v1 on v0

v1 whole, which is shorter than its diff:
```python
import jax
import jax.numpy as jnp
from jax import lax
from jax.experimental import pallas as pl
from jax.experimental.pallas import tpu as pltpu
from jax.sharding import PartitionSpec as P

MESH = pl.DeviceIdType.MESH
HALF = 64
OWN = 72
PAD = 8
MID = 16
ROWS = 96
F32 = jnp.float32
OFFSETS = ((1, 2), (1, 1), (1, 3), (0, 2), (1, 0), (0, 1), (0, 3))


def part(start, size):
    if not isinstance(start, int):
        start = pl.multiple_of(start, 8)
    return pl.ds(start, size)


def kernel(
    base_hbm, satur_hbm, mob_hbm, a_hbm, j_hbm, r_hbm, starts_hbm, ends_hbm,
    base_ref, satur_ref, mob_ref, in_a, in_j, in_r, ta, tj, tr, starts, drive, regions,
    coef_a, coef_b, mobile, gain, reluct, work, ends, corr0, items, got, sums, out_e, out_s,
    in_sem, pair_send, pair_recv, edge_send, edge_recv, reg_send, reg_recv,
    there_send, there_recv, back_send, back_recv, halo_send, halo_recv, out_send, out_recv, out_sem,
):
    tm = lax.axis_index("tm")
    sp = lax.axis_index("space")
    core = lax.rem(tm, 2)
    other = 1 - core
    pair = tm - core
    chip = tm // 2
    right = lax.rem(sp + 1, 16)
    left = lax.rem(sp + 15, 16)
    outer = jnp.where(core == 0, left, right)
    ahead = jnp.where(core == 0, right, left)

    def far(dy, dx):
        return 4 * lax.rem(chip // 4 + dy, 2) + lax.rem(lax.rem(chip, 4) + dx, 4)

    loads = []
    for n, (src, dst) in enumerate(
        ((r_hbm, in_r), (a_hbm, in_a), (j_hbm, in_j), (base_hbm, base_ref), (satur_hbm, satur_ref), (mob_hbm, mob_ref))
    ):
        cp = pltpu.make_async_copy(src, dst, in_sem.at[n])
        cp.start()
        loads.append(cp)

    barrier = pltpu.get_barrier_semaphore()
    for dy, dx in OFFSETS:
        pl.semaphore_signal(barrier, inc=1, device_id=(2 * far(dy, dx) + core, sp), device_id_type=MESH)
    pl.semaphore_signal(barrier, inc=1, device_id=(pair, outer), device_id_type=MESH)
    pl.semaphore_signal(barrier, inc=1, device_id=(pair + 1, outer), device_id_type=MESH)
    pl.semaphore_signal(barrier, inc=1, device_id=(pair + other, sp), device_id_type=MESH)

    def turn(src, dst):
        for t in range(8):
            dst[t] = src[pl.ds(t, 128, stride=8), :].T

    own = part(MID - PAD * core, OWN)
    mine = part((128 - OWN) * core, OWN)
    edge = part(jnp.where(core == 0, PAD, MID + HALF), 8)

    loads[0].wait()
    turn(in_r, tr)
    for cp in loads[3:]:
        cp.wait()
    base = [base_ref[k] for k in range(8)]
    satur = [satur_ref[k] for k in range(8)]
    full = lambda x: jnp.full((8, 128), x, F32)
    tab_a = [full(0.5 * b * (1.0 + s)) for b, s in zip(base, satur)]
    tab_b = [full(2.0 * b * s) for b, s in zip(base, satur)]
    tab_m = [full(mob_ref[k]) for k in range(8)]
    tab_c = [1.0 / (1.0 + 12.0 * m * full(b)) for b, m in zip(base, tab_m)]

    def look_up(src, first, at, size):
        for t in range(8):
            for k in range(size // 8):
                r = src[t, part(first + 8 * k, 8)]
                bits = [(r & 1) != 0, (r & 2) != 0, (r & 4) != 0]
                for tab, ref in ((tab_a, coef_a), (tab_b, coef_b), (tab_m, mobile), (tab_c, gain)):
                    level = tab
                    for bit in bits:
                        level = [jnp.where(bit, hi, lo) for lo, hi in zip(level[::2], level[1::2])]
                    ref[t, part(at + 8 * k, 8)] = level[0]

    look_up(tr, (128 - OWN) * core, MID - PAD * core, OWN)
    loads[1].wait()
    turn(in_a.at[0], ta)
    starts[0, core, :, own] = ta[:, mine]
    loads[2].wait()
    turn(in_j.at[0], tj)
    drive[core, :, own] = tj[:, mine]

    pl.semaphore_wait(barrier, 10)

    sends = []
    pairs = []
    for n, (src, dst) in enumerate(((ta, starts.at[0]), (tj, drive))):
        cp = pltpu.make_async_remote_copy(
            src.at[:, pl.ds(120, 8)], dst.at[core, :, pl.ds(PAD, 8)],
            edge_send.at[n, 0], edge_recv.at[n, core], device_id=(pair, right), device_id_type=MESH,
        )
        cp.start()
        sends.append(cp)
        cp = pltpu.make_async_remote_copy(
            src.at[:, pl.ds(0, 8)], dst.at[core, :, pl.ds(MID + HALF, 8)],
            edge_send.at[n, 1], edge_recv.at[n, core], device_id=(pair + 1, left), device_id_type=MESH,
        )
        cp.start()
        sends.append(cp)
        if n == 0:
            cp_reg = pltpu.make_async_remote_copy(
                tr.at[:, part(120 * other, 8)], regions.at[:, part(jnp.where(core == 0, 0, 8), 8)],
                reg_send, reg_recv, device_id=(tm, ahead), device_id_type=MESH,
            )
            cp_reg.start()
            sends.append(cp_reg)
        cp = pltpu.make_async_remote_copy(
            src.at[:, part((128 - OWN) * other, OWN)], dst.at[core, :, own_of(core)],
            pair_send.at[n], pair_recv.at[n], device_id=(pair + other, sp), device_id_type=MESH,
        )
        cp.start()
        pairs.append(cp)

    cp_reg.wait_recv()
    look_up(regions, jnp.where(core == 0, 0, 8), jnp.where(core == 0, PAD, MID + HALF), 8)

    lane = lambda size: lax.broadcasted_iota(jnp.int32, (size, 128), 1)

    def up(x, end):
        return jnp.where(lane(x.shape[0]) == 127, end, pltpu.roll(x, 127, 1))

    def down(x, end):
        return jnp.where(lane(x.shape[0]) == 0, end, pltpu.roll(x, 1, 1))

    def fine(src, dst, at, size, to):
        wide = pl.ds(PAD, 80)
        mid, east, west = pl.ds(at, size), pl.ds(at + 1, size), pl.ds(at - 1, size)
        out = pl.ds(to, size)
        for p in range(2):
            a = [src.at[p, t] for t in range(8)]
            for t in range(8):
                north = a[t + 1][wide] if t < 7 else up(a[0][wide], 0.0)
                south = a[t - 1][wide] if t > 0 else down(a[7][wide], 0.0)
                br = north - south
                bt = a[t][pl.ds(PAD + 1, 80)] - a[t][pl.ds(PAD - 1, 80)]
                reluct[t, wide] = coef_a[t, wide] - coef_b[t, wide] / (4.0 + (br * br + bt * bt))
            nu0, nu7, a0, a7 = reluct[0, mid], reluct[7, mid], a[0][mid], a[7][mid]
            top = (nu7 + up(nu0, nu7)) * (up(a0, 0.0) - a7)
            below = down(top, 2.0 * nu0 * a0)
            for t in range(8):
                nu, here = reluct[t, mid], a[t][mid]
                above = top if t == 7 else (nu + reluct[t + 1, mid]) * (a[t + 1][mid] - here)
                turned = (nu + reluct[t, east]) * (a[t][east] - here) + (nu + reluct[t, west]) * (a[t][west] - here)
                total = turned + (above - below) + drive[p, t, mid]
                dst[p, t, out] = here + mobile[t, mid] * total
                below = above

    for cp in pairs:
        cp.wait_recv()
    for n in range(2):
        for p in range(2):
            pltpu.make_async_remote_copy(
                ta.at[:, pl.ds(0, 8)], starts.at[0, 0, :, pl.ds(PAD, 8)],
                edge_send.at[n, 0], edge_recv.at[n, p], device_id=(tm, right), device_id_type=MESH,
            ).wait_recv()

    inner = pl.ds(MID, HALF)
    for it in range(2):
        fine(starts.at[it], work.at[0], PAD, 80, PAD)
        fine(work.at[0], work.at[1], PAD, 80, PAD)
        fine(work.at[1], ends.at[it], MID, HALF, 0)

        if it == 1:
            cp_e = pltpu.make_async_remote_copy(
                ends.at[1, other], out_e.at[:, part(HALF * core, HALF)],
                out_send.at[0], out_recv.at[0], device_id=(pair + other, sp), device_id_type=MESH,
            )
            cp_e.start()
            sends.append(cp_e)

        for t in range(8):
            c = gain[t, inner]
            e0, e1 = ends[it, 0, t], ends[it, 1, t]
            k0 = e0 - c * starts[it, 0, t, inner]
            k1 = e1 - c * starts[it, 1, t, inner]
            corr0[t] = k0
            items[it, t] = jnp.where(chip == 7, e1, c * k0 + k1)

        there = []
        for n, (dy, dx) in enumerate(OFFSETS):
            q = far(dy, dx)
            cp = pltpu.make_async_remote_copy(
                items.at[it, :, part(8 * q, 8)], got.at[it, chip],
                there_send.at[it, n], there_recv.at[it, n], device_id=(2 * q + core, sp), device_id_type=MESH,
            )
            cp.start()
            there.append(cp)
        got[it, chip] = items[it, :, part(8 * chip, 8)]
        c = gain[:, part(8 * chip + MID, 8)]
        c2 = c * c
        if it == 1:
            out_e[:, part(HALF * core, HALF)] = ends[1, core]
        for cp in there:
            cp.wait_recv()
        sends += there

        total = got[it, 7]
        sums[it, 0] = total
        for k in range(7):
            total = c2 * total + got[it, k]
            sums[it, k + 1] = total

        back = []
        for n, (dy, dx) in enumerate(OFFSETS):
            q = far(dy, dx)
            cp = pltpu.make_async_remote_copy(
                sums.at[it, q], starts.at[it + 1, 0, :, part(8 * chip + MID, 8)],
                back_send.at[it, n], back_recv.at[it, n], device_id=(2 * q + core, sp), device_id_type=MESH,
            )
            cp.start()
            back.append(cp)
        starts[it + 1, 0, :, part(8 * chip + MID, 8)] = sums[it, chip]
        if it == 1:
            cp_e.wait_recv()
            for t in range(8):
                in_a[0, pl.ds(t, 128, stride=8), :] = out_e[t].T
            store_e = pltpu.make_async_copy(in_a, ends_hbm, out_sem.at[0])
            store_e.start()
        for cp in back:
            cp.wait_recv()
        sends += back

        for t in range(8):
            starts[it + 1, 1, t, inner] = gain[t, inner] * starts[it + 1, 0, t, inner] + corr0[t]

        if it == 0:
            halos = []
            for n in range(2):
                if n == 0:
                    target = (jnp.where(core == 0, pair + 1, pair), jnp.where(core == 0, left, sp))
                    src, dst = pl.ds(MID, 8), pl.ds(MID + HALF, 8)
                else:
                    target = (jnp.where(core == 0, pair + 1, pair), jnp.where(core == 0, sp, right))
                    src, dst = pl.ds(MID + HALF - 8, 8), pl.ds(PAD, 8)
                cp = pltpu.make_async_remote_copy(
                    starts.at[1, :, :, src], starts.at[1, :, :, dst],
                    halo_send.at[n], halo_recv.at[n], device_id=target, device_id_type=MESH,
                )
                cp.start()
                halos.append(cp)
            for cp in halos:
                cp.wait_recv()
            sends += halos

    cp_s = pltpu.make_async_remote_copy(
        starts.at[2, other, :, inner], out_s.at[:, part(HALF * core, HALF)],
        out_send.at[1], out_recv.at[1], device_id=(pair + other, sp), device_id_type=MESH,
    )
    cp_s.start()
    sends.append(cp_s)
    out_s[:, part(HALF * core, HALF)] = starts[2, core, :, inner]
    cp_s.wait_recv()
    for t in range(8):
        in_j[0, pl.ds(t, 128, stride=8), :] = out_s[t].T
    store_s = pltpu.make_async_copy(in_j, starts_hbm, out_sem.at[1])
    store_s.start()
    for cp in sends + pairs:
        cp.wait_send()
    store_e.wait()
    store_s.wait()


def own_of(sender):
    return part(MID - PAD * (1 - sender), OWN)


def local(initial_starts, source, region, base_reluctivity, saturation, mobility):
    block = jax.ShapeDtypeStruct((1, 1024, 128), F32)
    hbm = pl.BlockSpec(memory_space=pltpu.HBM)
    vmem = lambda *shape: pltpu.VMEM(shape + (128,), F32)
    ints = lambda *shape: pltpu.VMEM(shape + (128,), jnp.int32)
    table = pltpu.SMEM((8,), F32)
    sem = lambda *shape: pltpu.SemaphoreType.DMA(shape)
    return pl.pallas_call(
        kernel,
        out_shape=(block, block),
        in_specs=[hbm] * 6,
        out_specs=(hbm, hbm),
        scratch_shapes=[
            table, table, table,
            vmem(1, 1024), vmem(1, 1024), ints(1024), vmem(8, 128), vmem(8, 128), ints(8, 128),
            vmem(3, 2, 8, ROWS), vmem(2, 8, ROWS), ints(8, 16),
            vmem(8, ROWS), vmem(8, ROWS), vmem(8, ROWS), vmem(8, ROWS), vmem(8, ROWS),
            vmem(2, 2, 8, ROWS), vmem(2, 2, 8, HALF), vmem(8, HALF), vmem(2, 8, HALF), vmem(2, 8, 8, 8), vmem(2, 8, 8, 8),
            vmem(8, 128), vmem(8, 128),
            sem(6), sem(2), sem(2), sem(2, 2), sem(2, 2), pltpu.SemaphoreType.DMA, pltpu.SemaphoreType.DMA,
            sem(2, 7), sem(2, 7), sem(2, 7), sem(2, 7), sem(2), sem(2), sem(2), sem(2), sem(2),
        ],
        compiler_params=pltpu.CompilerParams(
            collective_id=0, has_side_effects=True, vmem_limit_bytes=64 * 2**20
        ),
        name="parareal",
    )(base_reluctivity, saturation, mobility, initial_starts, source, region)


def solution(mesh):
    in_specs = (P("tm", None, "space"), P("tm", None, "space"), P(None, "space"), P(), P(), P())
    out_specs = (P("tm", None, "space"), P("tm", None, "space"))
    return jax.shard_map(local, mesh=mesh, in_specs=in_specs, out_specs=out_specs, check_vma=False)
```

time: 72.6 us -> 50.2 us (0.69)
  Pallas kernels: 65 us -> 46.7 us
  local copies, waits for them, and re-layouts: 6.67 us -> 2.72 us
    pallas_call x1, Pallas kernels: 65 us -> 46.7 us  [local(): pl.pallas_call(kernel, out_shape=(block, block), in_specs=[hbm] * 6, out_...]
    unnamed x14 -> x4, local copies, waits for them, and re-layouts: 6.67 us -> 2.72 us
where the time goes in v1:
time: 50.2 us; the launch traced here: 50.1 us
  Pallas kernels  46.7 us (93%)
  local copies, waits for them, and re-layouts  2.72 us (5%)
  between operations  0.65 us (1%)
    pallas_call x1, Pallas kernels, local(): pl.pallas_call(kernel, out_shape=(block, block), in_specs=[hbm] * 6, out_...  46.7 us
    unnamed x4, local copies, waits for them, and re-layouts  2.72 us

profile of v1, /device:TPU:1, one launch (start us, length us, event | category | flops | bytes accessed | tf_op | source)
XLA Modules:
  0.0 50.1 jit_solution(4037339874970435451)
XLA Ops:
  0.6 46.7 %parareal.1 = (f32[1,1024,128]{2,1,0:T(8,128)}, f32[1,1024,128]{2,1,0:T(8,128)}) custom-call(f32[8]{0:T(128)} %base_hbm.1, f32[8]{0:T(128)} %satur_hbm.1, f32[8]{0:T(128)} %mob_hbm.1, f32[1,1024,128]{2,1,0:T(8,128)} %a_hbm.1, f32[1,1024,128]{2,1,0:T(8,128)} %j_hbm.1, s32[1024,128]{1,0:T(8,128)} %r_hbm.1), custom_call_target="tpu_custom_call" | custom-call | tf_op jit(solution)/shard_map/parareal/pallas_call | solution.py:290
  47.4 0.0 copy-start
  47.4 1.9 %copy.10 = f32[1,1024,128]{2,1,0:T(8,128)} copy(f32[1,1024,128]{2,1,0:T(8,128)} %get-tuple-element.4) | data formatting | bytes 1048576
  49.3 0.0 copy-done
  49.3 0.8 %copy.11 = f32[1,1024,128]{2,1,0:T(8,128)} copy(f32[1,1024,128]{2,1,0:T(8,128)S(1)} %copy-done) | data formatting | bytes 1048576
Async XLA Ops:
  47.4 1.9 %copy-start = (f32[1,1024,128]{2,1,0:T(8,128)S(1)}, f32[1,1024,128]{2,1,0:T(8,128)}, u32[]{:S(2)}) copy-start(f32[1,1024,128]{2,1,0:T(8,128)} %get-tuple-element.5) | copy-start | bytes 1572868

commit v2 on v1

v2 whole, which is shorter than its diff:
```python
import jax
import jax.numpy as jnp
from jax import lax
from jax.experimental import pallas as pl
from jax.experimental.pallas import tpu as pltpu
from jax.sharding import PartitionSpec as P

MESH = pl.DeviceIdType.MESH
HALF = 64
OWN = 72
PAD = 8
MID = 16
ROWS = 96
EDGE = 40
F32 = jnp.float32
OFFSETS = ((1, 2), (1, 1), (1, 3), (0, 2), (1, 0), (0, 1), (0, 3))


def part(start, size):
    if not isinstance(start, int):
        start = pl.multiple_of(start, 8)
    return pl.ds(start, size)


def up(x, end):
    return jnp.where(lax.broadcasted_iota(jnp.int32, x.shape, 1) == 127, end, pltpu.roll(x, 127, 1))


def down(x, end):
    return jnp.where(lax.broadcasted_iota(jnp.int32, x.shape, 1) == 0, end, pltpu.roll(x, 1, 1))


def reluctivity(a, coef_a, coef_b, nu, at, size):
    rows = pl.ds(at, size)
    for t in range(8):
        north = a[t + 1][rows] if t < 7 else up(a[0][rows], 0.0)
        south = a[t - 1][rows] if t > 0 else down(a[7][rows], 0.0)
        br = north - south
        bt = a[t][pl.ds(at + 1, size)] - a[t][pl.ds(at - 1, size)]
        nu[t][rows] = coef_a[t, rows] - coef_b[t, rows] / (4.0 + (br * br + bt * bt))


def turning(a, nu, at, size):
    here, mid = a[pl.ds(at, size)], nu[pl.ds(at, size)]
    flux = (mid + nu[pl.ds(at + 1, size)]) * (a[pl.ds(at + 1, size)] - here)
    return flux + (mid + nu[pl.ds(at - 1, size)]) * (a[pl.ds(at - 1, size)] - here)


def update(a, nu, drive, mobile, at, size, put):
    rows = pl.ds(at, size)
    nu0, nu7, a0, a7 = nu[0][rows], nu[7][rows], a[0][rows], a[7][rows]
    top = (nu7 + up(nu0, nu7)) * (up(a0, 0.0) - a7)
    below = down(top, 2.0 * nu0 * a0)
    for t in range(8):
        here = a[t][rows]
        above = top if t == 7 else (nu[t][rows] + nu[t + 1][rows]) * (a[t + 1][rows] - here)
        total = turning(a[t], nu[t], at, size) + (above - below) + drive[t, rows]
        put(t, here + mobile[t, rows] * total)
        below = above


def kernel(
    base_hbm, satur_hbm, mob_hbm, a_hbm, j_hbm, r_hbm, out_s, out_e,
    base_ref, satur_ref, mob_ref, in_a, in_j, in_r, ta, tj, tr, starts, drive,
    coef_a, coef_b, mobile, gain, reluct, work, later,
    rim_r, rim, rim_drive, rim_a, rim_b, rim_mobile, rim_gain, rim_reluct, rim_work, rim_later, rim_items, rim_got,
    ends, corr0, items, got, sums,
    in_sem, pair_send, pair_recv, edge_send, edge_recv, reg_send, reg_recv,
    there_send, there_recv, back_send, back_recv, rim_send, rim_recv, halo_send, halo_recv,
    oute_send, oute_recv, outs_send, outs_recv,
):
    tm = lax.axis_index("tm")
    sp = lax.axis_index("space")
    core = lax.rem(tm, 2)
    other = 1 - core
    pair = tm - core
    chip = tm // 2
    right = lax.rem(sp + 1, 16)
    left = lax.rem(sp + 15, 16)
    outer = jnp.where(core == 0, left, right)
    partner = (pair + other, sp)
    beyond = (pair + other, outer)

    def far(dy, dx):
        return 4 * lax.rem(chip // 4 + dy, 2) + lax.rem(lax.rem(chip, 4) + dx, 4)

    def source(dy, dx):
        return far(dy, (4 - dx) % 4)

    def remote(src, dst, send, recv, target):
        return pltpu.make_async_remote_copy(src, dst, send, recv, device_id=target, device_id_type=MESH)

    loads = []
    for n, (src, dst) in enumerate(
        ((a_hbm, in_a), (j_hbm, in_j), (r_hbm, in_r), (base_hbm, base_ref), (satur_hbm, satur_ref), (mob_hbm, mob_ref))
    ):
        cp = pltpu.make_async_copy(src, dst, in_sem.at[n])
        cp.start()
        loads.append(cp)

    barrier = pltpu.get_barrier_semaphore()
    for dy, dx in OFFSETS:
        pl.semaphore_signal(barrier, inc=1, device_id=(2 * far(dy, dx) + core, sp), device_id_type=MESH)
    pl.semaphore_signal(barrier, inc=1, device_id=(pair, outer), device_id_type=MESH)
    pl.semaphore_signal(barrier, inc=1, device_id=(pair + 1, outer), device_id_type=MESH)
    pl.semaphore_signal(barrier, inc=1, device_id=partner, device_id_type=MESH)

    def turn(src, dst):
        for t in range(8):
            dst[t] = src[pl.ds(t, 128, stride=8), :].T

    sends = []

    def go(cp):
        cp.start()
        sends.append(cp)
        return cp

    own = part(MID - PAD * core, OWN)
    mine = part((128 - OWN) * core, OWN)
    theirs = part((128 - OWN) * other, OWN)
    theirs_at = part(MID - PAD * other, OWN)
    rim_halo = part(PAD + 16 * core, 8)
    rim_own = part(16 - 8 * core, 16)
    rim_from = part(MID + 48 * core, 16)
    far_halo = part(PAD + 72 * core, 8)
    rim_ends = part(56 * core, 8)

    loads[0].wait()
    turn(in_a.at[0], ta)
    pl.semaphore_wait(barrier, 10)

    def send_edges(n, src, dst):
        go(remote(src.at[:, pl.ds(120, 8)], dst.at[core, :, pl.ds(8, 8)], edge_send.at[n, 0], edge_recv.at[n, core], (pair, right)))
        go(remote(src.at[:, pl.ds(0, 8)], dst.at[core, :, pl.ds(24, 8)], edge_send.at[n, 1], edge_recv.at[n, core], (pair + 1, left)))

    send_edges(0, ta, rim)
    loads[1].wait()
    turn(in_j.at[0], tj)
    send_edges(1, tj, rim_drive)
    loads[2].wait()
    turn(in_r, tr)
    cp_reg = go(
        remote(tr.at[:, part(120 * other, 8)], rim_r.at[:, part(8 + 16 * core, 8)], reg_send, reg_recv, (tm, jnp.where(core == 0, right, left)))
    )
    pairs = [
        go(remote(src.at[:, theirs], dst.at[core, :, theirs_at], pair_send.at[n], pair_recv.at[n], partner))
        for n, (src, dst) in enumerate(((ta, starts.at[0]), (tj, drive)))
    ]

    for cp in loads[3:]:
        cp.wait()
    base = [base_ref[k] for k in range(8)]
    satur = [satur_ref[k] for k in range(8)]
    full = lambda x: jnp.full((8, 128), x, F32)
    tab_a = [full(0.5 * b * (1.0 + s)) for b, s in zip(base, satur)]
    tab_b = [full(2.0 * b * s) for b, s in zip(base, satur)]
    tab_m = [full(mob_ref[k]) for k in range(8)]
    tab_c = [1.0 / (1.0 + 12.0 * m * full(b)) for b, m in zip(base, tab_m)]

    def look_up(src, first, size, put):
        for t in range(8):
            for k in range(0, size, 8):
                r = src[t, part(first + k, 8)]
                bits = [(r & 1) != 0, (r & 2) != 0, (r & 4) != 0]
                for n, tab in enumerate((tab_a, tab_b, tab_m, tab_c)):
                    level = tab
                    for bit in bits:
                        level = [jnp.where(bit, hi, lo) for lo, hi in zip(level[::2], level[1::2])]
                    put(n, t, k, level[0])

    coefs = (coef_a, coef_b, mobile, gain)
    rim_coefs = (rim_a, rim_b, rim_mobile, rim_gain)

    def put_own(n, t, k, x):
        coefs[n][t, part(MID - PAD * core + k, 8)] = x

    def put_rim(n, t, k, x):
        rim_coefs[n][t, rim_halo] = x
        coefs[n][t, far_halo] = x

    look_up(tr, (128 - OWN) * core, OWN, put_own)
    starts[0, core, :, own] = ta[:, mine]
    drive[core, :, own] = tj[:, mine]

    inner = pl.ds(MID, HALF)
    chip7 = chip == 7

    def phases(ref):
        return [ref.at[t] for t in range(8)]

    nus = [reluct.at[t + 1] for t in range(8)]
    lates = [later.at[t + 1] for t in range(8)]

    def put_work(t, x):
        work[t, pl.ds(PAD, 80)] = x

    def put_later(t, x):
        later[t + 1, pl.ds(PAD, 80)] = x

    def two_steps(it, p):
        a = phases(starts.at[it, p])
        reluctivity(a, coef_a, coef_b, nus, PAD, 80)
        update(a, nus, drive.at[p], mobile, PAD, 80, put_work)
        a = phases(work)
        reluctivity(a, coef_a, coef_b, nus, PAD, 80)
        update(a, nus, drive.at[p], mobile, PAD, 80, put_later)
        reluctivity(lates, coef_a, coef_b, nus, PAD, 80)

    def last_step(p, t):
        here, mid = later[t + 1, inner], reluct[t + 1, inner]
        total = turning(later.at[t + 1], reluct.at[t + 1], MID, HALF) + drive[p, t, inner]
        total += (mid + reluct[t + 2, inner]) * (later[t + 2, inner] - here)
        total += (mid + reluct[t, inner]) * (later[t, inner] - here)
        return here + mobile[t, inner] * total

    for it in range(2):
        def put_ends(t, x):
            ends[it, core, t] = x
            if it == 1:
                out_e[t, part(HALF * core, HALF)] = x

        two_steps(it, core)
        update(lates, nus, drive.at[core], mobile, MID, HALF, put_ends)
        if it == 0:
            for cp in pairs:
                cp.wait_recv()
        two_steps(it, other)
        wide = pl.ds(PAD, 80)
        later[0, wide] = down(later[8, wide], 0.0)
        later[9, wide] = up(later[1, wide], 0.0)
        reluct[0, wide] = down(reluct[8, wide], reluct[1, wide])
        reluct[9, wide] = up(reluct[1, wide], reluct[8, wide])

        window = part(8 * other, 56) if it == 0 else pl.ds(0, HALF)
        frame_window = part(MID + 8 * other, 56) if it == 0 else inner

        def finish(t):
            theirs_end = last_step(other, t)
            ends[it, other, t] = theirs_end
            own_end = ends[it, core, t]
            c = gain[t, inner]
            own_corr = own_end - c * starts[it, core, t, inner]
            theirs_corr = theirs_end - c * starts[it, other, t, inner]
            first = jnp.where(core == 0, own_corr, theirs_corr)
            second = jnp.where(core == 0, theirs_corr, own_corr)
            corr0[it, t] = first
            items[it, t] = jnp.where(chip7, jnp.where(core == 0, theirs_end, own_end), c * first + second)

        there = []
        for n, (dy, dx) in enumerate(OFFSETS):
            q = far(dy, dx)
            finish(q)
            there.append(
                go(remote(items.at[it, q, window], got.at[it, chip, window], there_send.at[it, n], there_recv.at[it, n], (2 * q + core, sp)))
            )
        finish(chip)
        got[it, chip] = items[it, chip]

        if it == 1:
            cp_e = go(remote(ends.at[1, other], out_e.at[:, part(HALF * core, HALF)], oute_send, oute_recv, partner))
        else:
            cp_reg.wait_recv()
            look_up(rim_r, PAD + 16 * core, 8, put_rim)
            for ref, into in zip(coefs, rim_coefs):
                into[:, rim_own] = ref[:, rim_from]
            for n in range(2):
                for p in range(2):
                    remote(
                        ta.at[:, pl.ds(0, 8)], rim.at[0, :, pl.ds(8, 8)], edge_send.at[n, 0], edge_recv.at[n, p], partner
                    ).wait_recv()
            rim_nus = phases(rim_reluct)
            for p in range(2):
                rim[p, :, rim_own] = starts[0, p, :, rim_from]
                rim_drive[p, :, rim_own] = drive[p, :, rim_from]
                drive[p, :, far_halo] = rim_drive[p, :, rim_halo]

                def put_rim_work(t, x):
                    rim_work[t, pl.ds(8, 24)] = x

                def put_rim_later(t, x):
                    rim_later[t, pl.ds(8, 24)] = x

                def put_rim_ends(t, x):
                    ends[0, p, t, rim_ends] = x

                for a, put in ((rim.at[p], put_rim_work), (rim_work, put_rim_later)):
                    reluctivity(phases(a), rim_a, rim_b, rim_nus, 8, 24)
                    update(phases(a), rim_nus, rim_drive.at[p], rim_mobile, 8, 24, put)
                reluctivity(phases(rim_later), rim_a, rim_b, rim_nus, 8, 24)
                update(phases(rim_later), rim_nus, rim_drive.at[p], rim_mobile, 16, 8, put_rim_ends)
            rim_c = gain[:, part(MID + 56 * core, 8)]
            k0 = ends[0, 0, :, rim_ends] - rim_c * starts[0, 0, :, part(MID + 56 * core, 8)]
            k1 = ends[0, 1, :, rim_ends] - rim_c * starts[0, 1, :, part(MID + 56 * core, 8)]
            corr0[0, :, rim_ends] = k0
            rim_items[...] = jnp.where(chip7, ends[0, 1, :, rim_ends], rim_c * k0 + k1)
            rim_got[chip] = rim_items[...]

            def rim_copy(n):
                q = far(*OFFSETS[n])
                return remote(rim_items, rim_got.at[chip], rim_send.at[n], rim_recv.at[n], (2 * q + core, sp))

            for n, offset in enumerate(OFFSETS):
                @pl.when((far(*offset) > chip) | chip7)
                def _():
                    rim_copy(n).start()

        for cp in there:
            cp.wait_recv()
        c = gain[chip, frame_window]
        c2 = c * c
        total = got[it, 7, window]
        sums[it, 0, window] = total
        for k in range(7):
            total = c2 * total + got[it, k, window]
            sums[it, k + 1, window] = total
        back = []
        for n, (dy, dx) in enumerate(OFFSETS):
            q = far(dy, dx)
            back.append(
                go(remote(sums.at[it, q, window], starts.at[it + 1, 0, chip, frame_window], back_send.at[it, n], back_recv.at[it, n], (2 * q + core, sp)))
            )
        starts[it + 1, 0, chip, frame_window] = sums[it, chip, window]

        if it == 0:
            for n, (dy, dx) in enumerate(OFFSETS):
                @pl.when((source(dy, dx) < chip) | (source(dy, dx) == 7))
                def _():
                    rim_copy(n).wait_recv()
            rim_c2 = rim_c * rim_c
            total = rim_got[7]
            for k in range(7):
                total = jnp.where(k < chip, rim_c2 * total + rim_got[k], total)
            starts[1, 0, :, part(MID + 56 * core, 8)] = total
            starts[1, 1, :, part(MID + 56 * core, 8)] = rim_c * total + k0
            outer_halo = go(
                remote(starts.at[1, :, :, part(MID + 56 * core, 8)], starts.at[1, :, :, part(PAD + 72 * other, 8)], halo_send.at[0], halo_recv.at[0], beyond)
            )

        def spread(t):
            starts[it + 1, 1, t, frame_window] = gain[t, frame_window] * starts[it + 1, 0, t, frame_window] + corr0[it, t, window]

        if it == 0:
            spread(chip)
            for n in reversed(range(7)):
                back[n].wait_recv()
                spread(source(*OFFSETS[n]))
            inner_halo = go(
                remote(starts.at[1, :, :, part(MID + 56 * other, 8)], starts.at[1, :, :, part(PAD + 72 * core, 8)], halo_send.at[1], halo_recv.at[1], partner)
            )
            outer_halo.wait_recv()
            inner_halo.wait_recv()
        else:
            outs = []
            for n in reversed(range(8)):
                t = chip
                if n < 7:
                    back[n].wait_recv()
                    t = source(*OFFSETS[n])
                spread(t)
                outs.append(
                    go(remote(starts.at[2, other, t, inner], out_s.at[t, part(HALF * core, HALF)], outs_send.at[n], outs_recv.at[n], partner))
                )
                out_s[t, part(HALF * core, HALF)] = starts[2, core, t, inner]

    cp_e.wait_recv()
    for cp in outs:
        cp.wait_recv()
    for cp in sends:
        cp.wait_send()
    for n, offset in enumerate(OFFSETS):
        @pl.when((far(*offset) > chip) | chip7)
        def _():
            rim_copy(n).wait_send()


def hand_out(s_ref, e_ref, starts_hbm, ends_hbm, buf, sem):
    copies = []
    for n, (src, dst) in enumerate(((e_ref, ends_hbm), (s_ref, starts_hbm))):
        for t in range(8):
            buf[n, 0, pl.ds(t, 128, stride=8), :] = src[t].T
        cp = pltpu.make_async_copy(buf.at[n], dst, sem.at[n])
        cp.start()
        copies.append(cp)
    for cp in copies:
        cp.wait()


def local(initial_starts, source, region, base_reluctivity, saturation, mobility):
    held = jax.ShapeDtypeStruct((8, 128, 128), F32)
    block = jax.ShapeDtypeStruct((1, 1024, 128), F32)
    hbm = pl.BlockSpec(memory_space=pltpu.HBM)
    in_vmem = pl.BlockSpec(memory_space=pltpu.VMEM)
    vmem = lambda *shape: pltpu.VMEM(shape + (128,), F32)
    ints = lambda *shape: pltpu.VMEM(shape + (128,), jnp.int32)
    table = pltpu.SMEM((8,), F32)
    sem = lambda *shape: pltpu.SemaphoreType.DMA(shape)
    one = pltpu.SemaphoreType.DMA
    args = (base_reluctivity, saturation, mobility, initial_starts, source, region)
    kept = pl.pallas_call(
        kernel,
        out_shape=(held, held),
        in_specs=[hbm] * 6,
        out_specs=(in_vmem, in_vmem),
        scratch_shapes=[
            table, table, table,
            vmem(1, 1024), vmem(1, 1024), ints(1024), vmem(8, 128), vmem(8, 128), ints(8, 128),
            vmem(3, 2, 8, ROWS), vmem(2, 8, ROWS),
            vmem(8, ROWS), vmem(8, ROWS), vmem(8, ROWS), vmem(8, ROWS), vmem(10, ROWS), vmem(8, ROWS), vmem(10, ROWS),
            ints(8, EDGE), vmem(2, 8, EDGE), vmem(2, 8, EDGE), vmem(8, EDGE), vmem(8, EDGE), vmem(8, EDGE), vmem(8, EDGE),
            vmem(8, EDGE), vmem(8, EDGE), vmem(8, EDGE), vmem(8, 8), vmem(8, 8, 8),
            vmem(2, 2, 8, HALF), vmem(2, 8, HALF), vmem(2, 8, HALF), vmem(2, 8, HALF), vmem(2, 8, HALF),
            sem(6), sem(2), sem(2), sem(2, 2), sem(2, 2), one, one,
            sem(2, 7), sem(2, 7), sem(2, 7), sem(2, 7), sem(7), sem(7), sem(2), sem(2),
            one, one, sem(8), sem(8),
        ],
        compiler_params=pltpu.CompilerParams(
            collective_id=0, has_side_effects=True, vmem_limit_bytes=40 * 2**20
        ),
        name="parareal",
    )(*[pltpu.with_memory_space_constraint(x, pltpu.HBM) for x in args])
    return pl.pallas_call(
        hand_out,
        out_shape=(block, block),
        in_specs=[in_vmem] * 2,
        out_specs=(hbm, hbm),
        scratch_shapes=[vmem(2, 1, 1024), sem(2)],
        compiler_params=pltpu.CompilerParams(vmem_limit_bytes=16 * 2**20),
        name="hand_out",
    )(*kept)


def solution(mesh):
    in_specs = (P("tm", None, "space"), P("tm", None, "space"), P(None, "space"), P(), P(), P())
    out_specs = (P("tm", None, "space"), P("tm", None, "space"))
    return jax.shard_map(local, mesh=mesh, in_specs=in_specs, out_specs=out_specs, check_vma=False)
```

time: 50.2 us -> 43.3 us (0.86)
  Pallas kernels: 46.7 us -> 42.6 us
  local copies, waits for them, and re-layouts: 2.72 us -> 0 us
    pallas_call x1 -> x2, Pallas kernels: 46.7 us -> 42.6 us  [the longest x1 41.4 us: local(): pl.pallas_call(kernel, out_shape=(held, held), in_specs=[hbm] * 6, out_sp...]
    unnamed x4 -> x0, local copies, waits for them, and re-layouts: 2.72 us -> none
where the time goes in v2:
time: 43.3 us; the launch traced here: 43.2 us
  Pallas kernels  42.6 us (98%)
  between operations  0.64 us (1%)
    pallas_call x1, Pallas kernels, local(): pl.pallas_call(kernel, out_shape=(held, held), in_specs=[hbm] * 6, out_sp...  41.4 us
    pallas_call x1, Pallas kernels, local(): pl.pallas_call(hand_out, out_shape=(block, block), in_specs=[in_vmem] * 2...  1.19 us

profile of v2, /device:TPU:1, one launch (start us, length us, event | category | flops | bytes accessed | tf_op | source)
XLA Modules:
  0.0 43.2 jit_solution(16963462074173314826)
XLA Ops:
  0.6 41.4 %parareal.1 = (f32[8,128,128]{2,1,0:T(8,128)S(1)}, f32[8,128,128]{2,1,0:T(8,128)S(1)}) custom-call(f32[8]{0:T(128)} %base_hbm.1, f32[8]{0:T(128)} %satur_hbm.1, f32[8]{0:T(128)} %mob_hbm.1, f32[1,1024,128]{2,1,0:T(8,128)} %a_hbm.1, f32[1,1024,128]{2,1,0:T(8,128)} %j_hbm.1, s32[1024,128]{1,0:T(8,128)} %r_hbm.1), custom_call_target="tpu_custom_call" | custom-call | tf_op jit(solution)/shard_map/parareal/pallas_call | solution.py:400
  42.1 1.2 %hand_out.1 = (f32[1,1024,128]{2,1,0:T(8,128)}, f32[1,1024,128]{2,1,0:T(8,128)}) custom-call(f32[8,128,128]{2,1,0:T(8,128)S(1)} %get-tuple-element.4.s_ref, f32[8,128,128]{2,1,0:T(8,128)S(1)} %get-tuple-element.5.e_ref), custom_call_target="tpu_custom_call" | custom-call | tf_op jit(solution)/shard_map/hand_out/pallas_call | solution.py:422

commit v3 on v2

--- a/solution.py
+++ b/solution.py
@@ -7,11 +7,11 @@
 
 MESH = pl.DeviceIdType.MESH
 HALF = 64
-OWN = 72
+OWN = 80
 PAD = 8
 MID = 16
 ROWS = 96
-EDGE = 40
+EDGE = 48
 F32 = jnp.float32
 OFFSETS = ((1, 2), (1, 1), (1, 3), (0, 2), (1, 0), (0, 1), (0, 3))
 
@@ -63,10 +63,10 @@
     base_hbm, satur_hbm, mob_hbm, a_hbm, j_hbm, r_hbm, out_s, out_e,
     base_ref, satur_ref, mob_ref, in_a, in_j, in_r, ta, tj, tr, starts, drive,
     coef_a, coef_b, mobile, gain, reluct, work, later,
-    rim_r, rim, rim_drive, rim_a, rim_b, rim_mobile, rim_gain, rim_reluct, rim_work, rim_later, rim_items, rim_got,
+    rim_r, rim, rim_drive, rim_a, rim_b, rim_mobile, rim_gain, rim_reluct, rim_work, rim_later, rim_ends, rim_corr0, rim_items, rim_got,
     ends, corr0, items, got, sums,
     in_sem, pair_send, pair_recv, edge_send, edge_recv, reg_send, reg_recv,
-    there_send, there_recv, back_send, back_recv, rim_send, rim_recv, halo_send, halo_recv,
+    there_send, there_recv, back_send, back_recv, rim_send, rim_recv,
     oute_send, oute_recv, outs_send, outs_recv,
 ):
     tm = lax.axis_index("tm")
@@ -79,7 +79,6 @@
     left = lax.rem(sp + 15, 16)
     outer = jnp.where(core == 0, left, right)
     partner = (pair + other, sp)
-    beyond = (pair + other, outer)
 
     def far(dy, dx):
         return 4 * lax.rem(chip // 4 + dy, 2) + lax.rem(lax.rem(chip, 4) + dx, 4)
@@ -116,37 +115,41 @@
         sends.append(cp)
         return cp
 
-    own = part(MID - PAD * core, OWN)
+    wide = pl.ds(PAD, OWN)
+    inner = pl.ds(MID, HALF)
     mine = part((128 - OWN) * core, OWN)
     theirs = part((128 - OWN) * other, OWN)
-    theirs_at = part(MID - PAD * other, OWN)
-    rim_halo = part(PAD + 16 * core, 8)
-    rim_own = part(16 - 8 * core, 16)
-    rim_from = part(MID + 48 * core, 16)
-    far_halo = part(PAD + 72 * core, 8)
-    rim_ends = part(56 * core, 8)
+    rim_halo = part(8 + 16 * core, 16)
+    rim_own = part(8 + 16 * other, 16)
+    rim_from = part(PAD + 64 * core, 16)
+    rim_out = pl.ds(16, 16)
+    kept, kept_at = part(PAD + 8 * core, 72), part(PAD + 8 * other, 72)
+    beyond, beyond_at = part(16 + 8 * core, 8), part(PAD + 72 * core, 8)
+    back_at = part(PAD + 16 * other, 64)
+    rim_at = part(PAD + 64 * core, 16)
+    own_half = part(HALF * core, HALF)
 
     loads[0].wait()
     turn(in_a.at[0], ta)
     pl.semaphore_wait(barrier, 10)
 
     def send_edges(n, src, dst):
-        go(remote(src.at[:, pl.ds(120, 8)], dst.at[core, :, pl.ds(8, 8)], edge_send.at[n, 0], edge_recv.at[n, core], (pair, right)))
-        go(remote(src.at[:, pl.ds(0, 8)], dst.at[core, :, pl.ds(24, 8)], edge_send.at[n, 1], edge_recv.at[n, core], (pair + 1, left)))
+        go(remote(src.at[:, pl.ds(112, 16)], dst.at[core, :, pl.ds(8, 16)], edge_send.at[n, 0], edge_recv.at[n, core], (pair, right)))
+        go(remote(src.at[:, pl.ds(0, 16)], dst.at[core, :, pl.ds(24, 16)], edge_send.at[n, 1], edge_recv.at[n, core], (pair + 1, left)))
+
+    def send_pair(n, src, dst):
+        return go(remote(src.at[:, theirs], dst.at[core, :, wide], pair_send.at[n], pair_recv.at[n], partner))
 
     send_edges(0, ta, rim)
     loads[1].wait()
     turn(in_j.at[0], tj)
     send_edges(1, tj, rim_drive)
+    pairs = [send_pair(0, ta, starts.at[0]), send_pair(1, tj, drive.at[0])]
     loads[2].wait()
     turn(in_r, tr)
     cp_reg = go(
-        remote(tr.at[:, part(120 * other, 8)], rim_r.at[:, part(8 + 16 * core, 8)], reg_send, reg_recv, (tm, jnp.where(core == 0, right, left)))
+        remote(tr.at[:, part(112 * other, 16)], rim_r.at[:, rim_halo], reg_send, reg_recv, (tm, jnp.where(core == 0, right, left)))
     )
-    pairs = [
-        go(remote(src.at[:, theirs], dst.at[core, :, theirs_at], pair_send.at[n], pair_recv.at[n], partner))
-        for n, (src, dst) in enumerate(((ta, starts.at[0]), (tj, drive)))
-    ]
 
     for cp in loads[3:]:
         cp.wait()
@@ -173,17 +176,15 @@
     rim_coefs = (rim_a, rim_b, rim_mobile, rim_gain)
 
     def put_own(n, t, k, x):
-        coefs[n][t, part(MID - PAD * core + k, 8)] = x
+        coefs[n][0, t, pl.ds(PAD + k, 8)] = x
 
     def put_rim(n, t, k, x):
-        rim_coefs[n][t, rim_halo] = x
-        coefs[n][t, far_halo] = x
+        rim_coefs[n][t, part(8 + 16 * core + k, 8)] = x
 
     look_up(tr, (128 - OWN) * core, OWN, put_own)
-    starts[0, core, :, own] = ta[:, mine]
-    drive[core, :, own] = tj[:, mine]
-
-    inner = pl.ds(MID, HALF)
+    starts[0, core, :, wide] = ta[:, mine]
+    drive[0, core, :, wide] = tj[:, mine]
+
     chip7 = chip == 7
 
     def phases(ref):
@@ -193,53 +194,50 @@
     lates = [later.at[t + 1] for t in range(8)]
 
     def put_work(t, x):
-        work[t, pl.ds(PAD, 80)] = x
+        work[t, wide] = x
 
     def put_later(t, x):
-        later[t + 1, pl.ds(PAD, 80)] = x
+        later[t + 1, wide] = x
 
     def two_steps(it, p):
+        ca, cb, cm, force = coef_a.at[it], coef_b.at[it], mobile.at[it], drive.at[it, p]
         a = phases(starts.at[it, p])
-        reluctivity(a, coef_a, coef_b, nus, PAD, 80)
-        update(a, nus, drive.at[p], mobile, PAD, 80, put_work)
+        reluctivity(a, ca, cb, nus, PAD, OWN)
+        update(a, nus, force, cm, PAD, OWN, put_work)
         a = phases(work)
-        reluctivity(a, coef_a, coef_b, nus, PAD, 80)
-        update(a, nus, drive.at[p], mobile, PAD, 80, put_later)
-        reluctivity(lates, coef_a, coef_b, nus, PAD, 80)
-
-    def last_step(p, t):
+        reluctivity(a, ca, cb, nus, PAD, OWN)
+        update(a, nus, force, cm, PAD, OWN, put_later)
+        reluctivity(lates, ca, cb, nus, PAD, OWN)
+
+    def last_step(it, p, t):
         here, mid = later[t + 1, inner], reluct[t + 1, inner]
-        total = turning(later.at[t + 1], reluct.at[t + 1], MID, HALF) + drive[p, t, inner]
+        total = turning(later.at[t + 1], reluct.at[t + 1], MID, HALF) + drive[it, p, t, inner]
         total += (mid + reluct[t + 2, inner]) * (later[t + 2, inner] - here)
         total += (mid + reluct[t, inner]) * (later[t, inner] - here)
-        return here + mobile[t, inner] * total
+        return here + mobile[it, t, inner] * total
 
     for it in range(2):
         def put_ends(t, x):
             ends[it, core, t] = x
             if it == 1:
-                out_e[t, part(HALF * core, HALF)] = x
+                out_e[t, own_half] = x
 
         two_steps(it, core)
-        update(lates, nus, drive.at[core], mobile, MID, HALF, put_ends)
+        update(lates, nus, drive.at[it, core], mobile.at[it], MID, HALF, put_ends)
         if it == 0:
             for cp in pairs:
                 cp.wait_recv()
         two_steps(it, other)
-        wide = pl.ds(PAD, 80)
         later[0, wide] = down(later[8, wide], 0.0)
         later[9, wide] = up(later[1, wide], 0.0)
         reluct[0, wide] = down(reluct[8, wide], reluct[1, wide])
         reluct[9, wide] = up(reluct[1, wide], reluct[8, wide])
 
-        window = part(8 * other, 56) if it == 0 else pl.ds(0, HALF)
-        frame_window = part(MID + 8 * other, 56) if it == 0 else inner
-
         def finish(t):
-            theirs_end = last_step(other, t)
+            theirs_end = last_step(it, other, t)
             ends[it, other, t] = theirs_end
             own_end = ends[it, core, t]
-            c = gain[t, inner]
+            c = gain[it, t, inner]
             own_corr = own_end - c * starts[it, core, t, inner]
             theirs_corr = theirs_end - c * starts[it, other, t, inner]
             first = jnp.where(core == 0, own_corr, theirs_corr)
@@ -252,48 +250,47 @@
             q = far(dy, dx)
             finish(q)
             there.append(
-                go(remote(items.at[it, q, window], got.at[it, chip, window], there_send.at[it, n], there_recv.at[it, n], (2 * q + core, sp)))
+                go(remote(items.at[it, q], got.at[it, chip], there_send.at[it, n], there_recv.at[it, n], (2 * q + core, sp)))
             )
         finish(chip)
         got[it, chip] = items[it, chip]
 
         if it == 1:
-            cp_e = go(remote(ends.at[1, other], out_e.at[:, part(HALF * core, HALF)], oute_send, oute_recv, partner))
+            cp_e = go(remote(ends.at[1, other], out_e.at[:, own_half], oute_send, oute_recv, partner))
         else:
             cp_reg.wait_recv()
-            look_up(rim_r, PAD + 16 * core, 8, put_rim)
+            look_up(rim_r, 8 + 16 * core, 16, put_rim)
             for ref, into in zip(coefs, rim_coefs):
-                into[:, rim_own] = ref[:, rim_from]
+                into[:, rim_own] = ref[0, :, rim_from]
             for n in range(2):
                 for p in range(2):
                     remote(
-                        ta.at[:, pl.ds(0, 8)], rim.at[0, :, pl.ds(8, 8)], edge_send.at[n, 0], edge_recv.at[n, p], partner
+                        ta.at[:, pl.ds(0, 16)], rim.at[0, :, pl.ds(8, 16)], edge_send.at[n, 0], edge_recv.at[n, p], partner
                     ).wait_recv()
             rim_nus = phases(rim_reluct)
             for p in range(2):
                 rim[p, :, rim_own] = starts[0, p, :, rim_from]
-                rim_drive[p, :, rim_own] = drive[p, :, rim_from]
-                drive[p, :, far_halo] = rim_drive[p, :, rim_halo]
+                rim_drive[p, :, rim_own] = drive[0, p, :, rim_from]
 
                 def put_rim_work(t, x):
-                    rim_work[t, pl.ds(8, 24)] = x
+                    rim_work[t, pl.ds(8, 32)] = x
 
                 def put_rim_later(t, x):
-                    rim_later[t, pl.ds(8, 24)] = x
+                    rim_later[t, pl.ds(8, 32)] = x
 
                 def put_rim_ends(t, x):
-                    ends[0, p, t, rim_ends] = x
+                    rim_ends[p, t] = x
 
                 for a, put in ((rim.at[p], put_rim_work), (rim_work, put_rim_later)):
-                    reluctivity(phases(a), rim_a, rim_b, rim_nus, 8, 24)
-                    update(phases(a), rim_nus, rim_drive.at[p], rim_mobile, 8, 24, put)
-                reluctivity(phases(rim_later), rim_a, rim_b, rim_nus, 8, 24)
-                update(phases(rim_later), rim_nus, rim_drive.at[p], rim_mobile, 16, 8, put_rim_ends)
-            rim_c = gain[:, part(MID + 56 * core, 8)]
-            k0 = ends[0, 0, :, rim_ends] - rim_c * starts[0, 0, :, part(MID + 56 * core, 8)]
-            k1 = ends[0, 1, :, rim_ends] - rim_c * starts[0, 1, :, part(MID + 56 * core, 8)]
-            corr0[0, :, rim_ends] = k0
-            rim_items[...] = jnp.where(chip7, ends[0, 1, :, rim_ends], rim_c * k0 + k1)
+                    reluctivity(phases(a), rim_a, rim_b, rim_nus, 8, 32)
+                    update(phases(a), rim_nus, rim_drive.at[p], rim_mobile, 8, 32, put)
+                reluctivity(phases(rim_later), rim_a, rim_b, rim_nus, 8, 32)
+                update(phases(rim_later), rim_nus, rim_drive.at[p], rim_mobile, 16, 16, put_rim_ends)
+            rim_c = rim_gain[:, rim_out]
+            k0 = rim_ends[0] - rim_c * rim[0, :, rim_out]
+            k1 = rim_ends[1] - rim_c * rim[1, :, rim_out]
+            rim_corr0[...] = k0
+            rim_items[...] = jnp.where(chip7, rim_ends[1], rim_c * k0 + k1)
             rim_got[chip] = rim_items[...]
 
             def rim_copy(n):
@@ -305,51 +302,51 @@
                 def _():
                     rim_copy(n).start()
 
+            for ref, edge in zip(coefs, rim_coefs):
+                ref[1, :, kept_at] = ref[0, :, kept]
+                ref[1, :, beyond_at] = edge[:, beyond]
+            drive[1, :, :, kept_at] = drive[0, :, :, kept]
+            drive[1, :, :, beyond_at] = rim_drive[:, :, beyond]
+
         for cp in there:
             cp.wait_recv()
-        c = gain[chip, frame_window]
+        c = gain[it, chip, inner]
         c2 = c * c
-        total = got[it, 7, window]
-        sums[it, 0, window] = total
+        total = got[it, 7]
+        sums[it, 0] = total
         for k in range(7):
-            total = c2 * total + got[it, k, window]
-            sums[it, k + 1, window] = total
+            total = c2 * total + got[it, k]
+            sums[it, k + 1] = total
+        land = back_at if it == 0 else inner
         back = []
         for n, (dy, dx) in enumerate(OFFSETS):
             q = far(dy, dx)
             back.append(
-                go(remote(sums.at[it, q, window], starts.at[it + 1, 0, chip, frame_window], back_send.at[it, n], back_recv.at[it, n], (2 * q + core, sp)))
+                go(remote(sums.at[it, q], starts.at[it + 1, 0, chip, land], back_send.at[it, n], back_recv.at[it, n], (2 * q + core, sp)))
             )
-        starts[it + 1, 0, chip, frame_window] = sums[it, chip, window]
+        starts[it + 1, 0, chip, land] = sums[it, chip]
 
         if it == 0:
             for n, (dy, dx) in enumerate(OFFSETS):
                 @pl.when((source(dy, dx) < chip) | (source(dy, dx) == 7))
                 def _():
                     rim_copy(n).wait_recv()
+            rim_c = rim_gain[:, rim_out]
             rim_c2 = rim_c * rim_c
             total = rim_got[7]
             for k in range(7):
                 total = jnp.where(k < chip, rim_c2 * total + rim_got[k], total)
-            starts[1, 0, :, part(MID + 56 * core, 8)] = total
-            starts[1, 1, :, part(MID + 56 * core, 8)] = rim_c * total + k0
-            outer_halo = go(
-                remote(starts.at[1, :, :, part(MID + 56 * core, 8)], starts.at[1, :, :, part(PAD + 72 * other, 8)], halo_send.at[0], halo_recv.at[0], beyond)
-            )
+            starts[1, 0, :, rim_at] = total
+            starts[1, 1, :, rim_at] = rim_c * total + rim_corr0[...]
 
         def spread(t):
-            starts[it + 1, 1, t, frame_window] = gain[t, frame_window] * starts[it + 1, 0, t, frame_window] + corr0[it, t, window]
+            starts[it + 1, 1, t, land] = gain[it, t, inner] * starts[it + 1, 0, t, land] + corr0[it, t]
 
         if it == 0:
             spread(chip)
             for n in reversed(range(7)):
                 back[n].wait_recv()
                 spread(source(*OFFSETS[n]))
-            inner_halo = go(
-                remote(starts.at[1, :, :, part(MID + 56 * other, 8)], starts.at[1, :, :, part(PAD + 72 * core, 8)], halo_send.at[1], halo_recv.at[1], partner)
-            )
-            outer_halo.wait_recv()
-            inner_halo.wait_recv()
         else:
             outs = []
             for n in reversed(range(8)):
@@ -359,9 +356,9 @@
                     t = source(*OFFSETS[n])
                 spread(t)
                 outs.append(
-                    go(remote(starts.at[2, other, t, inner], out_s.at[t, part(HALF * core, HALF)], outs_send.at[n], outs_recv.at[n], partner))
+                    go(remote(starts.at[2, other, t, inner], out_s.at[t, own_half], outs_send.at[n], outs_recv.at[n], partner))
                 )
-                out_s[t, part(HALF * core, HALF)] = starts[2, core, t, inner]
+                out_s[t, own_half] = starts[2, core, t, inner]
 
     cp_e.wait_recv()
     for cp in outs:
@@ -405,13 +402,13 @@
         scratch_shapes=[
             table, table, table,
             vmem(1, 1024), vmem(1, 1024), ints(1024), vmem(8, 128), vmem(8, 128), ints(8, 128),
-            vmem(3, 2, 8, ROWS), vmem(2, 8, ROWS),
-            vmem(8, ROWS), vmem(8, ROWS), vmem(8, ROWS), vmem(8, ROWS), vmem(10, ROWS), vmem(8, ROWS), vmem(10, ROWS),
+            vmem(3, 2, 8, ROWS), vmem(2, 2, 8, ROWS),
+            vmem(2, 8, ROWS), vmem(2, 8, ROWS), vmem(2, 8, ROWS), vmem(2, 8, ROWS), vmem(10, ROWS), vmem(8, ROWS), vmem(10, ROWS),
             ints(8, EDGE), vmem(2, 8, EDGE), vmem(2, 8, EDGE), vmem(8, EDGE), vmem(8, EDGE), vmem(8, EDGE), vmem(8, EDGE),
-            vmem(8, EDGE), vmem(8, EDGE), vmem(8, EDGE), vmem(8, 8), vmem(8, 8, 8),
+            vmem(8, EDGE), vmem(8, EDGE), vmem(8, EDGE), vmem(2, 8, 16), vmem(8, 16), vmem(8, 16), vmem(8, 8, 16),
             vmem(2, 2, 8, HALF), vmem(2, 8, HALF), vmem(2, 8, HALF), vmem(2, 8, HALF), vmem(2, 8, HALF),
             sem(6), sem(2), sem(2), sem(2, 2), sem(2, 2), one, one,
-            sem(2, 7), sem(2, 7), sem(2, 7), sem(2, 7), sem(7), sem(7), sem(2), sem(2),
+            sem(2, 7), sem(2, 7), sem(2, 7), sem(2, 7), sem(7), sem(7),
             one, one, sem(8), sem(8),
         ],
         compiler_params=pltpu.CompilerParams(

time: 43.3 us -> 45 us (1.039)
  Pallas kernels: 42.6 us -> 44.3 us
    pallas_call x1, Pallas kernels: 41.4 us -> 43.1 us  [local(): pl.pallas_call(kernel, out_shape=(held, held), in_specs=[hbm] * 6, out_sp...]
where the time goes in v3:
time: 45 us; the launch traced here: 44.9 us
  Pallas kernels  44.3 us (98%)
  between operations  0.64 us (1%)
    pallas_call x1, Pallas kernels, local(): pl.pallas_call(kernel, out_shape=(held, held), in_specs=[hbm] * 6, out_sp...  43.1 us
    pallas_call x1, Pallas kernels, local(): pl.pallas_call(hand_out, out_shape=(block, block), in_specs=[in_vmem] * 2...  1.19 us

profile of v3, /device:TPU:1, one launch (start us, length us, event | category | flops | bytes accessed | tf_op | source)
XLA Modules:
  0.0 44.9 jit_solution(1557737163986259466)
XLA Ops:
  0.6 43.1 %parareal.1 = (f32[8,128,128]{2,1,0:T(8,128)S(1)}, f32[8,128,128]{2,1,0:T(8,128)S(1)}) custom-call(f32[8]{0:T(128)} %base_hbm.1, f32[8]{0:T(128)} %satur_hbm.1, f32[8]{0:T(128)} %mob_hbm.1, f32[1,1024,128]{2,1,0:T(8,128)} %a_hbm.1, f32[1,1024,128]{2,1,0:T(8,128)} %j_hbm.1, s32[1024,128]{1,0:T(8,128)} %r_hbm.1), custom_call_target="tpu_custom_call" | custom-call | tf_op jit(solution)/shard_map/parareal/pallas_call | solution.py:397
  43.7 1.2 %hand_out.1 = (f32[1,1024,128]{2,1,0:T(8,128)}, f32[1,1024,128]{2,1,0:T(8,128)}) custom-call(f32[8,128,128]{2,1,0:T(8,128)S(1)} %get-tuple-element.4.s_ref, f32[8,128,128]{2,1,0:T(8,128)S(1)} %get-tuple-element.5.e_ref), custom_call_target="tpu_custom_call" | custom-call | tf_op jit(solution)/shard_map/hand_out/pallas_call | solution.py:419

commit v4 on v3

--- a/solution.py
+++ b/solution.py
@@ -11,7 +11,7 @@
 PAD = 8
 MID = 16
 ROWS = 96
-EDGE = 48
+EDGE = 40
 F32 = jnp.float32
 OFFSETS = ((1, 2), (1, 1), (1, 3), (0, 2), (1, 0), (0, 1), (0, 3))
 
@@ -62,11 +62,11 @@
 def kernel(
     base_hbm, satur_hbm, mob_hbm, a_hbm, j_hbm, r_hbm, out_s, out_e,
     base_ref, satur_ref, mob_ref, in_a, in_j, in_r, ta, tj, tr, starts, drive,
-    coef_a, coef_b, mobile, gain, reluct, work, later,
+    coef_a, coef_b, mobile, gain, carry_gain, reluct, work, later,
     rim_r, rim, rim_drive, rim_a, rim_b, rim_mobile, rim_gain, rim_reluct, rim_work, rim_later, rim_ends, rim_corr0, rim_items, rim_got,
     ends, corr0, items, got, sums,
     in_sem, pair_send, pair_recv, edge_send, edge_recv, reg_send, reg_recv,
-    there_send, there_recv, back_send, back_recv, rim_send, rim_recv,
+    there_send, there_recv, back_send, back_recv, rim_send, rim_recv, halo_send, halo_recv,
     oute_send, oute_recv, outs_send, outs_recv,
 ):
     tm = lax.axis_index("tm")
@@ -90,16 +90,27 @@
         return pltpu.make_async_remote_copy(src, dst, send, recv, device_id=target, device_id_type=MESH)
 
     loads = []
-    for n, (src, dst) in enumerate(
-        ((a_hbm, in_a), (j_hbm, in_j), (r_hbm, in_r), (base_hbm, base_ref), (satur_hbm, satur_ref), (mob_hbm, mob_ref))
-    ):
-        cp = pltpu.make_async_copy(src, dst, in_sem.at[n])
+    for n, (src, dst, pieces) in enumerate(((a_hbm.at[0], in_a.at[0], 4), (j_hbm.at[0], in_j.at[0], 4), (r_hbm, in_r, 4))):
+        size = 1024 // pieces
+        loads.append([])
+        for k in range(pieces):
+            cp = pltpu.make_async_copy(src.at[pl.ds(size * k, size)], dst.at[pl.ds(size * k, size)], in_sem.at[n, k])
+            cp.start()
+            loads[-1].append(cp)
+    tables = []
+    for n, (src, dst) in enumerate(((base_hbm, base_ref), (satur_hbm, satur_ref), (mob_hbm, mob_ref))):
+        cp = pltpu.make_async_copy(src, dst, in_sem.at[3, n])
         cp.start()
-        loads.append(cp)
+        tables.append(cp)
+
+    def arrived(copies):
+        for cp in copies:
+            cp.wait()
 
     barrier = pltpu.get_barrier_semaphore()
     for dy, dx in OFFSETS:
         pl.semaphore_signal(barrier, inc=1, device_id=(2 * far(dy, dx) + core, sp), device_id_type=MESH)
+        pl.semaphore_signal(barrier, inc=1, device_id=(2 * far(dy, dx) + other, sp), device_id_type=MESH)
     pl.semaphore_signal(barrier, inc=1, device_id=(pair, outer), device_id_type=MESH)
     pl.semaphore_signal(barrier, inc=1, device_id=(pair + 1, outer), device_id_type=MESH)
     pl.semaphore_signal(barrier, inc=1, device_id=partner, device_id_type=MESH)
@@ -119,40 +130,39 @@
     inner = pl.ds(MID, HALF)
     mine = part((128 - OWN) * core, OWN)
     theirs = part((128 - OWN) * other, OWN)
-    rim_halo = part(8 + 16 * core, 16)
-    rim_own = part(8 + 16 * other, 16)
+    rim_halo = part(8 + 16 * core, 8)
+    rim_own = part(8 + 8 * other, 16)
     rim_from = part(PAD + 64 * core, 16)
-    rim_out = pl.ds(16, 16)
+    rim_out = pl.ds(16, 8)
     kept, kept_at = part(PAD + 8 * core, 72), part(PAD + 8 * other, 72)
-    beyond, beyond_at = part(16 + 8 * core, 8), part(PAD + 72 * core, 8)
-    back_at = part(PAD + 16 * other, 64)
-    rim_at = part(PAD + 64 * core, 16)
+    beyond_at = part(PAD + 72 * core, 8)
+    rim_at = part(MID + 56 * core, 8)
     own_half = part(HALF * core, HALF)
-
-    loads[0].wait()
+    own_half = part(HALF * core, HALF)
+
+    arrived(loads[0])
     turn(in_a.at[0], ta)
-    pl.semaphore_wait(barrier, 10)
+    pl.semaphore_wait(barrier, 17)
 
     def send_edges(n, src, dst):
-        go(remote(src.at[:, pl.ds(112, 16)], dst.at[core, :, pl.ds(8, 16)], edge_send.at[n, 0], edge_recv.at[n, core], (pair, right)))
-        go(remote(src.at[:, pl.ds(0, 16)], dst.at[core, :, pl.ds(24, 16)], edge_send.at[n, 1], edge_recv.at[n, core], (pair + 1, left)))
+        go(remote(src.at[:, pl.ds(120, 8)], dst.at[core, :, pl.ds(8, 8)], edge_send.at[n, 0], edge_recv.at[n, core], (pair, right)))
+        go(remote(src.at[:, pl.ds(0, 8)], dst.at[core, :, pl.ds(24, 8)], edge_send.at[n, 1], edge_recv.at[n, core], (pair + 1, left)))
 
     def send_pair(n, src, dst):
         return go(remote(src.at[:, theirs], dst.at[core, :, wide], pair_send.at[n], pair_recv.at[n], partner))
 
     send_edges(0, ta, rim)
-    loads[1].wait()
+    arrived(loads[1])
     turn(in_j.at[0], tj)
     send_edges(1, tj, rim_drive)
-    pairs = [send_pair(0, ta, starts.at[0]), send_pair(1, tj, drive.at[0])]
-    loads[2].wait()
+    arrived(loads[2])
     turn(in_r, tr)
     cp_reg = go(
-        remote(tr.at[:, part(112 * other, 16)], rim_r.at[:, rim_halo], reg_send, reg_recv, (tm, jnp.where(core == 0, right, left)))
+        remote(tr.at[:, part(120 * other, 8)], rim_r.at[:, rim_halo], reg_send, reg_recv, (tm, jnp.where(core == 0, right, left)))
     )
-
-    for cp in loads[3:]:
-        cp.wait()
+    pairs = [send_pair(0, ta, starts.at[0]), send_pair(1, tj, drive.at[0])]
+
+    arrived(tables)
     base = [base_ref[k] for k in range(8)]
     satur = [satur_ref[k] for k in range(8)]
     full = lambda x: jnp.full((8, 128), x, F32)
@@ -179,9 +189,16 @@
         coefs[n][0, t, pl.ds(PAD + k, 8)] = x
 
     def put_rim(n, t, k, x):
-        rim_coefs[n][t, part(8 + 16 * core + k, 8)] = x
+        rim_coefs[n][t, rim_halo] = x
 
     look_up(tr, (128 - OWN) * core, OWN, put_own)
+    for it, first in enumerate((8 + 48 * other, HALF * other)):
+        for k in range(0, HALF, 8):
+            r = tr[chip, part(first + k, 8)]
+            level = tab_c
+            for bit in ((r & 1) != 0, (r & 2) != 0, (r & 4) != 0):
+                level = [jnp.where(bit, hi, lo) for lo, hi in zip(level[::2], level[1::2])]
+            carry_gain[it, pl.ds(k, 8)] = level[0]
     starts[0, core, :, wide] = ta[:, mine]
     drive[0, core, :, wide] = tj[:, mine]
 
@@ -250,22 +267,22 @@
             q = far(dy, dx)
             finish(q)
             there.append(
-                go(remote(items.at[it, q], got.at[it, chip], there_send.at[it, n], there_recv.at[it, n], (2 * q + core, sp)))
+                go(remote(items.at[it, q], got.at[it, chip], there_send.at[it, n], there_recv.at[it, n], (2 * q + other, sp)))
             )
         finish(chip)
-        got[it, chip] = items[it, chip]
+        there.append(go(remote(items.at[it, chip], got.at[it, chip], there_send.at[it, 7], there_recv.at[it, 7], partner)))
 
         if it == 1:
             cp_e = go(remote(ends.at[1, other], out_e.at[:, own_half], oute_send, oute_recv, partner))
         else:
             cp_reg.wait_recv()
-            look_up(rim_r, 8 + 16 * core, 16, put_rim)
+            look_up(rim_r, 8 + 16 * core, 8, put_rim)
             for ref, into in zip(coefs, rim_coefs):
                 into[:, rim_own] = ref[0, :, rim_from]
             for n in range(2):
                 for p in range(2):
                     remote(
-                        ta.at[:, pl.ds(0, 16)], rim.at[0, :, pl.ds(8, 16)], edge_send.at[n, 0], edge_recv.at[n, p], partner
+                        ta.at[:, pl.ds(0, 8)], rim.at[0, :, pl.ds(8, 8)], edge_send.at[n, 0], edge_recv.at[n, p], partner
                     ).wait_recv()
             rim_nus = phases(rim_reluct)
             for p in range(2):
@@ -273,19 +290,19 @@
                 rim_drive[p, :, rim_own] = drive[0, p, :, rim_from]
 
                 def put_rim_work(t, x):
-                    rim_work[t, pl.ds(8, 32)] = x
+                    rim_work[t, pl.ds(8, 24)] = x
 
                 def put_rim_later(t, x):
-                    rim_later[t, pl.ds(8, 32)] = x
+                    rim_later[t, pl.ds(8, 24)] = x
 
                 def put_rim_ends(t, x):
                     rim_ends[p, t] = x
 
                 for a, put in ((rim.at[p], put_rim_work), (rim_work, put_rim_later)):
-                    reluctivity(phases(a), rim_a, rim_b, rim_nus, 8, 32)
-                    update(phases(a), rim_nus, rim_drive.at[p], rim_mobile, 8, 32, put)
-                reluctivity(phases(rim_later), rim_a, rim_b, rim_nus, 8, 32)
-                update(phases(rim_later), rim_nus, rim_drive.at[p], rim_mobile, 16, 16, put_rim_ends)
+                    reluctivity(phases(a), rim_a, rim_b, rim_nus, 8, 24)
+                    update(phases(a), rim_nus, rim_drive.at[p], rim_mobile, 8, 24, put)
+                reluctivity(phases(rim_later), rim_a, rim_b, rim_nus, 8, 24)
+                update(phases(rim_later), rim_nus, rim_drive.at[p], rim_mobile, 16, 8, put_rim_ends)
             rim_c = rim_gain[:, rim_out]
             k0 = rim_ends[0] - rim_c * rim[0, :, rim_out]
             k1 = rim_ends[1] - rim_c * rim[1, :, rim_out]
@@ -304,27 +321,28 @@
 
             for ref, edge in zip(coefs, rim_coefs):
                 ref[1, :, kept_at] = ref[0, :, kept]
-                ref[1, :, beyond_at] = edge[:, beyond]
+                ref[1, :, beyond_at] = edge[:, rim_halo]
             drive[1, :, :, kept_at] = drive[0, :, :, kept]
-            drive[1, :, :, beyond_at] = rim_drive[:, :, beyond]
+            drive[1, :, :, beyond_at] = rim_drive[:, :, rim_halo]
 
         for cp in there:
             cp.wait_recv()
-        c = gain[it, chip, inner]
+        c = carry_gain[it]
         c2 = c * c
         total = got[it, 7]
         sums[it, 0] = total
         for k in range(7):
             total = c2 * total + got[it, k]
             sums[it, k + 1] = total
-        land = back_at if it == 0 else inner
+        land = part(PAD + 16 * other, HALF) if it == 0 else inner
+        their_land = part(PAD + 16 * core, HALF) if it == 0 else inner
         back = []
         for n, (dy, dx) in enumerate(OFFSETS):
             q = far(dy, dx)
             back.append(
-                go(remote(sums.at[it, q], starts.at[it + 1, 0, chip, land], back_send.at[it, n], back_recv.at[it, n], (2 * q + core, sp)))
+                go(remote(sums.at[it, q], starts.at[it + 1, 0, chip, their_land], back_send.at[it, n], back_recv.at[it, n], (2 * q + other, sp)))
             )
-        starts[it + 1, 0, chip, land] = sums[it, chip]
+        back.append(go(remote(sums.at[it, chip], starts.at[it + 1, 0, chip, their_land], back_send.at[it, 7], back_recv.at[it, 7], partner)))
 
         if it == 0:
             for n, (dy, dx) in enumerate(OFFSETS):
@@ -338,22 +356,23 @@
                 total = jnp.where(k < chip, rim_c2 * total + rim_got[k], total)
             starts[1, 0, :, rim_at] = total
             starts[1, 1, :, rim_at] = rim_c * total + rim_corr0[...]
+            outer_halo = go(
+                remote(starts.at[1, :, :, rim_at], starts.at[1, :, :, part(PAD + 72 * other, 8)], halo_send, halo_recv, (pair + other, outer))
+            )
 
         def spread(t):
             starts[it + 1, 1, t, land] = gain[it, t, inner] * starts[it + 1, 0, t, land] + corr0[it, t]
 
         if it == 0:
-            spread(chip)
-            for n in reversed(range(7)):
+            for n in reversed(range(8)):
                 back[n].wait_recv()
-                spread(source(*OFFSETS[n]))
+                spread(source(*OFFSETS[n]) if n < 7 else chip)
+            outer_halo.wait_recv()
         else:
             outs = []
             for n in reversed(range(8)):
-                t = chip
-                if n < 7:
-                    back[n].wait_recv()
-                    t = source(*OFFSETS[n])
+                back[n].wait_recv()
+                t = source(*OFFSETS[n]) if n < 7 else chip
                 spread(t)
                 outs.append(
                     go(remote(starts.at[2, other, t, inner], out_s.at[t, own_half], outs_send.at[n], outs_recv.at[n], partner))
@@ -403,12 +422,12 @@
             table, table, table,
             vmem(1, 1024), vmem(1, 1024), ints(1024), vmem(8, 128), vmem(8, 128), ints(8, 128),
             vmem(3, 2, 8, ROWS), vmem(2, 2, 8, ROWS),
-            vmem(2, 8, ROWS), vmem(2, 8, ROWS), vmem(2, 8, ROWS), vmem(2, 8, ROWS), vmem(10, ROWS), vmem(8, ROWS), vmem(10, ROWS),
+            vmem(2, 8, ROWS), vmem(2, 8, ROWS), vmem(2, 8, ROWS), vmem(2, 8, ROWS), vmem(2, HALF), vmem(10, ROWS), vmem(8, ROWS), vmem(10, ROWS),
             ints(8, EDGE), vmem(2, 8, EDGE), vmem(2, 8, EDGE), vmem(8, EDGE), vmem(8, EDGE), vmem(8, EDGE), vmem(8, EDGE),
-            vmem(8, EDGE), vmem(8, EDGE), vmem(8, EDGE), vmem(2, 8, 16), vmem(8, 16), vmem(8, 16), vmem(8, 8, 16),
+            vmem(8, EDGE), vmem(8, EDGE), vmem(8, EDGE), vmem(2, 8, 8), vmem(8, 8), vmem(8, 8), vmem(8, 8, 8),
             vmem(2, 2, 8, HALF), vmem(2, 8, HALF), vmem(2, 8, HALF), vmem(2, 8, HALF), vmem(2, 8, HALF),
-            sem(6), sem(2), sem(2), sem(2, 2), sem(2, 2), one, one,
-            sem(2, 7), sem(2, 7), sem(2, 7), sem(2, 7), sem(7), sem(7),
+            sem(4, 4), sem(2), sem(2), sem(2, 2), sem(2, 2), one, one,
+            sem(2, 8), sem(2, 8), sem(2, 8), sem(2, 8), sem(7), sem(7), one, one,
             one, one, sem(8), sem(8),
         ],
         compiler_params=pltpu.CompilerParams(

time: 45 us -> 43.4 us (0.964)
  Pallas kernels: 44.3 us -> 42.6 us
    pallas_call x1, Pallas kernels: 43.1 us -> 41.4 us  [local(): pl.pallas_call(kernel, out_shape=(held, held), in_specs=[hbm] * 6, out_sp...]
where the time goes in v4:
time: 43.4 us; the launch traced here: 43.3 us
  Pallas kernels  42.6 us (98%)
  between operations  0.64 us (1%)
    pallas_call x1, Pallas kernels, local(): pl.pallas_call(kernel, out_shape=(held, held), in_specs=[hbm] * 6, out_sp...  41.4 us
    pallas_call x1, Pallas kernels, local(): pl.pallas_call(hand_out, out_shape=(block, block), in_specs=[in_vmem] * 2...  1.19 us

profile of v4, /device:TPU:1, one launch (start us, length us, event | category | flops | bytes accessed | tf_op | source)
XLA Modules:
  0.0 43.3 jit_solution(4883867747983103718)
XLA Ops:
  0.6 41.4 %parareal.1 = (f32[8,128,128]{2,1,0:T(8,128)S(1)}, f32[8,128,128]{2,1,0:T(8,128)S(1)}) custom-call(f32[8]{0:T(128)} %base_hbm.1, f32[8]{0:T(128)} %satur_hbm.1, f32[8]{0:T(128)} %mob_hbm.1, f32[1,1024,128]{2,1,0:T(8,128)} %a_hbm.1, f32[1,1024,128]{2,1,0:T(8,128)} %j_hbm.1, s32[1024,128]{1,0:T(8,128)} %r_hbm.1), custom_call_target="tpu_custom_call" | custom-call | tf_op jit(solution)/shard_map/parareal/pallas_call | solution.py:416
  42.1 1.2 %hand_out.1 = (f32[1,1024,128]{2,1,0:T(8,128)}, f32[1,1024,128]{2,1,0:T(8,128)}) custom-call(f32[8,128,128]{2,1,0:T(8,128)S(1)} %get-tuple-element.4.s_ref, f32[8,128,128]{2,1,0:T(8,128)S(1)} %get-tuple-element.5.e_ref), custom_call_target="tpu_custom_call" | custom-call | tf_op jit(solution)/shard_map/hand_out/pallas_call | solution.py:438

commit v5 on v4

--- a/solution.py
+++ b/solution.py
@@ -65,7 +65,7 @@
     coef_a, coef_b, mobile, gain, carry_gain, reluct, work, later,
     rim_r, rim, rim_drive, rim_a, rim_b, rim_mobile, rim_gain, rim_reluct, rim_work, rim_later, rim_ends, rim_corr0, rim_items, rim_got,
     ends, corr0, items, got, sums,
-    in_sem, pair_send, pair_recv, edge_send, edge_recv, reg_send, reg_recv,
+    word, in_sem, pair_send, pair_recv, edge_send, edge_recv, reg_send, reg_recv,
     there_send, there_recv, back_send, back_recv, rim_send, rim_recv, halo_send, halo_recv,
     oute_send, oute_recv, outs_send, outs_recv,
 ):
@@ -89,6 +89,12 @@
     def remote(src, dst, send, recv, target):
         return pltpu.make_async_remote_copy(src, dst, send, recv, device_id=target, device_id_type=MESH)
 
+    barrier = pltpu.get_barrier_semaphore()
+    across = (2 * far(1, 0) + core, sp)
+    near = [(2 * far(0, dx) + core, sp) for dx in (1, 3, 2)] + [across, (pair, outer), (pair + 1, outer), partner]
+    for device in near:
+        pl.semaphore_signal(barrier, inc=1, device_id=device, device_id_type=MESH)
+
     loads = []
     for n, (src, dst, pieces) in enumerate(((a_hbm.at[0], in_a.at[0], 4), (j_hbm.at[0], in_j.at[0], 4), (r_hbm, in_r, 4))):
         size = 1024 // pieces
@@ -107,14 +113,6 @@
         for cp in copies:
             cp.wait()
 
-    barrier = pltpu.get_barrier_semaphore()
-    for dy, dx in OFFSETS:
-        pl.semaphore_signal(barrier, inc=1, device_id=(2 * far(dy, dx) + core, sp), device_id_type=MESH)
-        pl.semaphore_signal(barrier, inc=1, device_id=(2 * far(dy, dx) + other, sp), device_id_type=MESH)
-    pl.semaphore_signal(barrier, inc=1, device_id=(pair, outer), device_id_type=MESH)
-    pl.semaphore_signal(barrier, inc=1, device_id=(pair + 1, outer), device_id_type=MESH)
-    pl.semaphore_signal(barrier, inc=1, device_id=partner, device_id_type=MESH)
-
     def turn(src, dst):
         for t in range(8):
             dst[t] = src[pl.ds(t, 128, stride=8), :].T
@@ -142,26 +140,11 @@
 
     arrived(loads[0])
     turn(in_a.at[0], ta)
-    pl.semaphore_wait(barrier, 17)
-
-    def send_edges(n, src, dst):
-        go(remote(src.at[:, pl.ds(120, 8)], dst.at[core, :, pl.ds(8, 8)], edge_send.at[n, 0], edge_recv.at[n, core], (pair, right)))
-        go(remote(src.at[:, pl.ds(0, 8)], dst.at[core, :, pl.ds(24, 8)], edge_send.at[n, 1], edge_recv.at[n, core], (pair + 1, left)))
-
-    def send_pair(n, src, dst):
-        return go(remote(src.at[:, theirs], dst.at[core, :, wide], pair_send.at[n], pair_recv.at[n], partner))
-
-    send_edges(0, ta, rim)
+
     arrived(loads[1])
     turn(in_j.at[0], tj)
-    send_edges(1, tj, rim_drive)
     arrived(loads[2])
     turn(in_r, tr)
-    cp_reg = go(
-        remote(tr.at[:, part(120 * other, 8)], rim_r.at[:, rim_halo], reg_send, reg_recv, (tm, jnp.where(core == 0, right, left)))
-    )
-    pairs = [send_pair(0, ta, starts.at[0]), send_pair(1, tj, drive.at[0])]
-
     arrived(tables)
     base = [base_ref[k] for k in range(8)]
     satur = [satur_ref[k] for k in range(8)]
@@ -202,6 +185,24 @@
     starts[0, core, :, wide] = ta[:, mine]
     drive[0, core, :, wide] = tj[:, mine]
 
+    pl.semaphore_wait(barrier, len(near))
+    pl.semaphore_signal(word.at[0], inc=1, device_id=across, device_id_type=MESH)
+
+    def send_edges(n, src, dst):
+        go(remote(src.at[:, pl.ds(120, 8)], dst.at[core, :, pl.ds(8, 8)], edge_send.at[n, 0], edge_recv.at[n, core], (pair, right)))
+        go(remote(src.at[:, pl.ds(0, 8)], dst.at[core, :, pl.ds(24, 8)], edge_send.at[n, 1], edge_recv.at[n, core], (pair + 1, left)))
+
+    def send_pair(n, src, dst):
+        return go(remote(src.at[:, theirs], dst.at[core, :, wide], pair_send.at[n], pair_recv.at[n], partner))
+
+    send_edges(0, ta, rim)
+    send_edges(1, tj, rim_drive)
+    cp_reg = go(
+        remote(tr.at[:, part(120 * other, 8)], rim_r.at[:, rim_halo], reg_send, reg_recv, (tm, jnp.where(core == 0, right, left)))
+    )
+    pairs = [send_pair(0, ta, starts.at[0]), send_pair(1, tj, drive.at[0])]
+
+
     chip7 = chip == 7
 
     def phases(ref):
@@ -242,6 +243,8 @@
         two_steps(it, core)
         update(lates, nus, drive.at[it, core], mobile.at[it], MID, HALF, put_ends)
         if it == 0:
+            pl.semaphore_wait(word.at[0], 1)
+            pl.semaphore_signal(word.at[1], inc=1, device_id=partner, device_id_type=MESH)
             for cp in pairs:
                 cp.wait_recv()
         two_steps(it, other)
@@ -262,6 +265,8 @@
             corr0[it, t] = first
             items[it, t] = jnp.where(chip7, jnp.where(core == 0, theirs_end, own_end), c * first + second)
 
+        if it == 0:
+            pl.semaphore_wait(word.at[1], 1)
         there = []
         for n, (dy, dx) in enumerate(OFFSETS):
             q = far(dy, dx)
@@ -426,7 +431,7 @@
             ints(8, EDGE), vmem(2, 8, EDGE), vmem(2, 8, EDGE), vmem(8, EDGE), vmem(8, EDGE), vmem(8, EDGE), vmem(8, EDGE),
             vmem(8, EDGE), vmem(8, EDGE), vmem(8, EDGE), vmem(2, 8, 8), vmem(8, 8), vmem(8, 8), vmem(8, 8, 8),
             vmem(2, 2, 8, HALF), vmem(2, 8, HALF), vmem(2, 8, HALF), vmem(2, 8, HALF), vmem(2, 8, HALF),
-            sem(4, 4), sem(2), sem(2), sem(2, 2), sem(2, 2), one, one,
+            pltpu.SemaphoreType.REGULAR((2,)), sem(4, 4), sem(2), sem(2), sem(2, 2), sem(2, 2), one, one,
             sem(2, 8), sem(2, 8), sem(2, 8), sem(2, 8), sem(7), sem(7), one, one,
             one, one, sem(8), sem(8),
         ],

time: 43.4 us -> 42.6 us (0.982)
  Pallas kernels: 42.6 us -> 41.9 us
    pallas_call x1, Pallas kernels: 41.4 us -> 40.7 us  [local(): pl.pallas_call(kernel, out_shape=(held, held), in_specs=[hbm] * 6, out_sp...]
where the time goes in v5:
time: 42.6 us; the launch traced here: 42.5 us
  Pallas kernels  41.9 us (98%)
  between operations  0.64 us (2%)
    pallas_call x1, Pallas kernels, local(): pl.pallas_call(kernel, out_shape=(held, held), in_specs=[hbm] * 6, out_sp...  40.7 us
    pallas_call x1, Pallas kernels, local(): pl.pallas_call(hand_out, out_shape=(block, block), in_specs=[in_vmem] * 2...  1.19 us

profile of v5, /device:TPU:1, one launch (start us, length us, event | category | flops | bytes accessed | tf_op | source)
XLA Modules:
  0.0 42.5 jit_solution(2136854006784533916)
XLA Ops:
  0.6 40.7 %parareal.1 = (f32[8,128,128]{2,1,0:T(8,128)S(1)}, f32[8,128,128]{2,1,0:T(8,128)S(1)}) custom-call(f32[8]{0:T(128)} %base_hbm.1, f32[8]{0:T(128)} %satur_hbm.1, f32[8]{0:T(128)} %mob_hbm.1, f32[1,1024,128]{2,1,0:T(8,128)} %a_hbm.1, f32[1,1024,128]{2,1,0:T(8,128)} %j_hbm.1, s32[1024,128]{1,0:T(8,128)} %r_hbm.1), custom_call_target="tpu_custom_call" | custom-call | tf_op jit(solution)/shard_map/parareal/pallas_call | solution.py:421
  41.3 1.2 %hand_out.1 = (f32[1,1024,128]{2,1,0:T(8,128)}, f32[1,1024,128]{2,1,0:T(8,128)}) custom-call(f32[8,128,128]{2,1,0:T(8,128)S(1)} %get-tuple-element.4.s_ref, f32[8,128,128]{2,1,0:T(8,128)S(1)} %get-tuple-element.5.e_ref), custom_call_target="tpu_custom_call" | custom-call | tf_op jit(solution)/shard_map/hand_out/pallas_call | solution.py:443

commit v6 on v5

--- a/solution.py
+++ b/solution.py
@@ -30,33 +30,43 @@
     return jnp.where(lax.broadcasted_iota(jnp.int32, x.shape, 1) == 0, end, pltpu.roll(x, 1, 1))
 
 
+def blocks(at, size):
+    step = size // 2 if size >= 64 else size
+    return [(at + k, step) for k in range(0, size, step)]
+
+
 def reluctivity(a, coef_a, coef_b, nu, at, size):
-    rows = pl.ds(at, size)
-    for t in range(8):
-        north = a[t + 1][rows] if t < 7 else up(a[0][rows], 0.0)
-        south = a[t - 1][rows] if t > 0 else down(a[7][rows], 0.0)
-        br = north - south
-        bt = a[t][pl.ds(at + 1, size)] - a[t][pl.ds(at - 1, size)]
-        nu[t][rows] = coef_a[t, rows] - coef_b[t, rows] / (4.0 + (br * br + bt * bt))
-
-
-def turning(a, nu, at, size):
-    here, mid = a[pl.ds(at, size)], nu[pl.ds(at, size)]
+    for start, step in blocks(at, size):
+        rows = pl.ds(start, step)
+        here = [x[rows] for x in a]
+        for t in range(8):
+            north = here[t + 1] if t < 7 else up(here[0], 0.0)
+            south = here[t - 1] if t > 0 else down(here[7], 0.0)
+            br = north - south
+            bt = a[t][pl.ds(start + 1, step)] - a[t][pl.ds(start - 1, step)]
+            nu[t][rows] = coef_a[t, rows] - coef_b[t, rows] / (4.0 + (br * br + bt * bt))
+
+
+def turning(a, nu, here, mid, at, size):
     flux = (mid + nu[pl.ds(at + 1, size)]) * (a[pl.ds(at + 1, size)] - here)
     return flux + (mid + nu[pl.ds(at - 1, size)]) * (a[pl.ds(at - 1, size)] - here)
 
 
 def update(a, nu, drive, mobile, at, size, put):
-    rows = pl.ds(at, size)
-    nu0, nu7, a0, a7 = nu[0][rows], nu[7][rows], a[0][rows], a[7][rows]
-    top = (nu7 + up(nu0, nu7)) * (up(a0, 0.0) - a7)
-    below = down(top, 2.0 * nu0 * a0)
-    for t in range(8):
-        here = a[t][rows]
-        above = top if t == 7 else (nu[t][rows] + nu[t + 1][rows]) * (a[t + 1][rows] - here)
-        total = turning(a[t], nu[t], at, size) + (above - below) + drive[t, rows]
-        put(t, here + mobile[t, rows] * total)
-        below = above
+    for start, step in blocks(at, size):
+        rows = pl.ds(start, step)
+        mid, nu7, here, a7 = nu[0][rows], nu[7][rows], a[0][rows], a[7][rows]
+        top = (nu7 + up(mid, nu7)) * (up(here, 0.0) - a7)
+        below = down(top, 2.0 * mid * here)
+        for t in range(8):
+            if t < 7:
+                following, next_nu = a[t + 1][rows], nu[t + 1][rows]
+                above = (mid + next_nu) * (following - here)
+            else:
+                above = top
+            total = turning(a[t], nu[t], here, mid, start, step) + (above - below) + drive[t, rows]
+            put(t, pl.ds(start - at, step), here + mobile[t, rows] * total)
+            below, here, mid = above, following, next_nu
 
 
 def kernel(
@@ -90,8 +100,8 @@
         return pltpu.make_async_remote_copy(src, dst, send, recv, device_id=target, device_id_type=MESH)
 
     barrier = pltpu.get_barrier_semaphore()
-    across = (2 * far(1, 0) + core, sp)
-    near = [(2 * far(0, dx) + core, sp) for dx in (1, 3, 2)] + [across, (pair, outer), (pair + 1, outer), partner]
+    tellers = [(2 * far(1, 0) + core, sp), (2 * far(1, 0) + other, sp), partner]
+    near = [(2 * far(0, dx) + core, sp) for dx in (1, 3, 2)] + tellers
     for device in near:
         pl.semaphore_signal(barrier, inc=1, device_id=device, device_id_type=MESH)
 
@@ -133,9 +143,8 @@
     rim_from = part(PAD + 64 * core, 16)
     rim_out = pl.ds(16, 8)
     kept, kept_at = part(PAD + 8 * core, 72), part(PAD + 8 * other, 72)
-    beyond_at = part(PAD + 72 * core, 8)
+    window, their_window = part(8 * other, 56), part(8 * core, 56)
     rim_at = part(MID + 56 * core, 8)
-    own_half = part(HALF * core, HALF)
     own_half = part(HALF * core, HALF)
 
     arrived(loads[0])
@@ -185,23 +194,48 @@
     starts[0, core, :, wide] = ta[:, mine]
     drive[0, core, :, wide] = tj[:, mine]
 
-    pl.semaphore_wait(barrier, len(near))
-    pl.semaphore_signal(word.at[0], inc=1, device_id=across, device_id_type=MESH)
-
-    def send_edges(n, src, dst):
-        go(remote(src.at[:, pl.ds(120, 8)], dst.at[core, :, pl.ds(8, 8)], edge_send.at[n, 0], edge_recv.at[n, core], (pair, right)))
-        go(remote(src.at[:, pl.ds(0, 8)], dst.at[core, :, pl.ds(24, 8)], edge_send.at[n, 1], edge_recv.at[n, core], (pair + 1, left)))
+    even = lax.rem(sp, 2) == 0
+    edge_sources = [(pair, outer), (pair + 1, outer)]
+
+    def greet(devices):
+        for device in devices:
+            pl.semaphore_signal(barrier, inc=1, device_id=device, device_id_type=MESH)
+
+    @pl.when(even)
+    def _():
+        pl.semaphore_wait(barrier, len(near))
+        greet(edge_sources + [(tm, jnp.where(core == 0, right, left))])
+
+    @pl.when(jnp.logical_not(even))
+    def _():
+        pl.semaphore_wait(barrier, len(near) + 3)
+        greet(edge_sources)
+
+    for device in tellers:
+        pl.semaphore_signal(word, inc=1, device_id=device, device_id_type=MESH)
+
+    def edge_copies():
+        copies = []
+        for n, (src, dst) in enumerate(((ta, rim.at[0]), (tj, rim_drive))):
+            copies.append(
+                remote(src.at[:, pl.ds(120, 8)], dst.at[core, :, pl.ds(8, 8)], edge_send.at[n, 0], edge_recv.at[n, core], (pair, right))
+            )
+            copies.append(
+                remote(src.at[:, pl.ds(0, 8)], dst.at[core, :, pl.ds(24, 8)], edge_send.at[n, 1], edge_recv.at[n, core], (pair + 1, left))
+            )
+        ahead = (tm, jnp.where(core == 0, right, left))
+        copies.append(remote(tr.at[:, part(120 * other, 8)], rim_r.at[:, rim_halo], reg_send, reg_recv, ahead))
+        return copies
 
     def send_pair(n, src, dst):
         return go(remote(src.at[:, theirs], dst.at[core, :, wide], pair_send.at[n], pair_recv.at[n], partner))
 
-    send_edges(0, ta, rim)
-    send_edges(1, tj, rim_drive)
-    cp_reg = go(
-        remote(tr.at[:, part(120 * other, 8)], rim_r.at[:, rim_halo], reg_send, reg_recv, (tm, jnp.where(core == 0, right, left)))
-    )
+    @pl.when(jnp.logical_not(even))
+    def _():
+        for cp in edge_copies():
+            cp.start()
+
     pairs = [send_pair(0, ta, starts.at[0]), send_pair(1, tj, drive.at[0])]
-
 
     chip7 = chip == 7
 
@@ -211,11 +245,11 @@
     nus = [reluct.at[t + 1] for t in range(8)]
     lates = [later.at[t + 1] for t in range(8)]
 
-    def put_work(t, x):
-        work[t, wide] = x
-
-    def put_later(t, x):
-        later[t + 1, wide] = x
+    def put_work(t, rows, x):
+        work[t, pl.ds(PAD + rows.start, rows.size)] = x
+
+    def put_later(t, rows, x):
+        later[t + 1, pl.ds(PAD + rows.start, rows.size)] = x
 
     def two_steps(it, p):
         ca, cb, cm, force = coef_a.at[it], coef_b.at[it], mobile.at[it], drive.at[it, p]
@@ -229,22 +263,20 @@
 
     def last_step(it, p, t):
         here, mid = later[t + 1, inner], reluct[t + 1, inner]
-        total = turning(later.at[t + 1], reluct.at[t + 1], MID, HALF) + drive[it, p, t, inner]
+        total = turning(later.at[t + 1], reluct.at[t + 1], here, mid, MID, HALF) + drive[it, p, t, inner]
         total += (mid + reluct[t + 2, inner]) * (later[t + 2, inner] - here)
         total += (mid + reluct[t, inner]) * (later[t, inner] - here)
         return here + mobile[it, t, inner] * total
 
     for it in range(2):
-        def put_ends(t, x):
-            ends[it, core, t] = x
+        def put_ends(t, rows, x):
+            ends[it, core, t, rows] = x
             if it == 1:
-                out_e[t, own_half] = x
+                out_e[t, part(HALF * core + rows.start, rows.size)] = x
 
         two_steps(it, core)
         update(lates, nus, drive.at[it, core], mobile.at[it], MID, HALF, put_ends)
         if it == 0:
-            pl.semaphore_wait(word.at[0], 1)
-            pl.semaphore_signal(word.at[1], inc=1, device_id=partner, device_id_type=MESH)
             for cp in pairs:
                 cp.wait_recv()
         two_steps(it, other)
@@ -266,69 +298,81 @@
             items[it, t] = jnp.where(chip7, jnp.where(core == 0, theirs_end, own_end), c * first + second)
 
         if it == 0:
-            pl.semaphore_wait(word.at[1], 1)
+            pl.semaphore_wait(word, len(tellers))
         there = []
         for n, (dy, dx) in enumerate(OFFSETS):
             q = far(dy, dx)
             finish(q)
+            mine_out = items.at[it, q] if it == 0 else items.at[it, q, window]
             there.append(
-                go(remote(items.at[it, q], got.at[it, chip], there_send.at[it, n], there_recv.at[it, n], (2 * q + other, sp)))
+                go(remote(mine_out, got.at[it, chip] if it == 0 else got.at[it, chip, window], there_send.at[it, n], there_recv.at[it, n], (2 * q + other, sp)))
             )
         finish(chip)
-        there.append(go(remote(items.at[it, chip], got.at[it, chip], there_send.at[it, 7], there_recv.at[it, 7], partner)))
-
-        if it == 1:
-            cp_e = go(remote(ends.at[1, other], out_e.at[:, own_half], oute_send, oute_recv, partner))
-        else:
-            cp_reg.wait_recv()
+        mine_out = items.at[it, chip] if it == 0 else items.at[it, chip, window]
+        land = got.at[it, chip] if it == 0 else got.at[it, chip, window]
+        there.append(go(remote(mine_out, land, there_send.at[it, 7], there_recv.at[it, 7], partner)))
+
+        if it == 0:
+            @pl.when(even)
+            def _():
+                pl.semaphore_wait(barrier, 2)
+                for cp in edge_copies():
+                    cp.start()
+
+            edge_copies()[-1].wait_recv()
             look_up(rim_r, 8 + 16 * core, 8, put_rim)
             for ref, into in zip(coefs, rim_coefs):
                 into[:, rim_own] = ref[0, :, rim_from]
             for n in range(2):
                 for p in range(2):
                     remote(
-                        ta.at[:, pl.ds(0, 8)], rim.at[0, :, pl.ds(8, 8)], edge_send.at[n, 0], edge_recv.at[n, p], partner
+                        ta.at[:, pl.ds(0, 8)], rim.at[0, 0, :, pl.ds(8, 8)], edge_send.at[n, 0], edge_recv.at[n, p], partner
                     ).wait_recv()
-            rim_nus = phases(rim_reluct)
-            for p in range(2):
-                rim[p, :, rim_own] = starts[0, p, :, rim_from]
-                rim_drive[p, :, rim_own] = drive[0, p, :, rim_from]
-
-                def put_rim_work(t, x):
-                    rim_work[t, pl.ds(8, 24)] = x
-
-                def put_rim_later(t, x):
-                    rim_later[t, pl.ds(8, 24)] = x
-
-                def put_rim_ends(t, x):
-                    rim_ends[p, t] = x
-
-                for a, put in ((rim.at[p], put_rim_work), (rim_work, put_rim_later)):
-                    reluctivity(phases(a), rim_a, rim_b, rim_nus, 8, 24)
-                    update(phases(a), rim_nus, rim_drive.at[p], rim_mobile, 8, 24, put)
-                reluctivity(phases(rim_later), rim_a, rim_b, rim_nus, 8, 24)
-                update(phases(rim_later), rim_nus, rim_drive.at[p], rim_mobile, 16, 8, put_rim_ends)
-            rim_c = rim_gain[:, rim_out]
-            k0 = rim_ends[0] - rim_c * rim[0, :, rim_out]
-            k1 = rim_ends[1] - rim_c * rim[1, :, rim_out]
-            rim_corr0[...] = k0
-            rim_items[...] = jnp.where(chip7, rim_ends[1], rim_c * k0 + k1)
-            rim_got[chip] = rim_items[...]
-
-            def rim_copy(n):
-                q = far(*OFFSETS[n])
-                return remote(rim_items, rim_got.at[chip], rim_send.at[n], rim_recv.at[n], (2 * q + core, sp))
-
-            for n, offset in enumerate(OFFSETS):
-                @pl.when((far(*offset) > chip) | chip7)
-                def _():
-                    rim_copy(n).start()
-
-            for ref, edge in zip(coefs, rim_coefs):
+            rim_drive[:, :, rim_own] = drive[0, :, :, rim_from]
+            rim[0, :, :, rim_own] = starts[0, :, :, rim_from]
+        else:
+            outer_halo.wait_recv()
+            rim[1, :, :, rim_own] = starts[1, :, :, part(MID + 48 * core, 16)]
+        rim_nus = phases(rim_reluct)
+        for p in range(2):
+            def put_rim_work(t, rows, x):
+                rim_work[t, pl.ds(8, 24)] = x
+
+            def put_rim_later(t, rows, x):
+                rim_later[t, pl.ds(8, 24)] = x
+
+            def put_rim_ends(t, rows, x):
+                rim_ends[p, t] = x
+
+            for a, put in ((rim.at[it, p], put_rim_work), (rim_work, put_rim_later)):
+                reluctivity(phases(a), rim_a, rim_b, rim_nus, 8, 24)
+                update(phases(a), rim_nus, rim_drive.at[p], rim_mobile, 8, 24, put)
+            reluctivity(phases(rim_later), rim_a, rim_b, rim_nus, 8, 24)
+            update(phases(rim_later), rim_nus, rim_drive.at[p], rim_mobile, 16, 8, put_rim_ends)
+        rim_c = rim_gain[:, rim_out]
+        k0 = rim_ends[0] - rim_c * rim[it, 0, :, rim_out]
+        k1 = rim_ends[1] - rim_c * rim[it, 1, :, rim_out]
+        rim_corr0[...] = k0
+        rim_items[it] = jnp.where(chip7, rim_ends[1], rim_c * k0 + k1)
+        rim_got[it, chip] = rim_items[it]
+
+        def rim_copy(it, n):
+            q = far(*OFFSETS[n])
+            return remote(rim_items.at[it], rim_got.at[it, chip], rim_send.at[it, n], rim_recv.at[it, n], (2 * q + core, sp))
+
+        for n, offset in enumerate(OFFSETS):
+            @pl.when((far(*offset) > chip) | chip7)
+            def _():
+                rim_copy(it, n).start()
+
+        if it == 1:
+            ends[1, other, :, part(56 * core, 8)] = rim_ends[other]
+            out_e[:, part(120 * core, 8)] = rim_ends[core]
+            cp_e = go(remote(ends.at[1, other], out_e.at[:, own_half], oute_send, oute_recv, partner))
+        else:
+            for ref in coefs:
                 ref[1, :, kept_at] = ref[0, :, kept]
-                ref[1, :, beyond_at] = edge[:, rim_halo]
             drive[1, :, :, kept_at] = drive[0, :, :, kept]
-            drive[1, :, :, beyond_at] = rim_drive[:, :, rim_halo]
 
         for cp in there:
             cp.wait_recv()
@@ -339,51 +383,60 @@
         for k in range(7):
             total = c2 * total + got[it, k]
             sums[it, k + 1] = total
-        land = part(PAD + 16 * other, HALF) if it == 0 else inner
-        their_land = part(PAD + 16 * core, HALF) if it == 0 else inner
+        rows = pl.ds(0, HALF) if it == 0 else window
+        their_rows = pl.ds(0, HALF) if it == 0 else their_window
+        frame_rows = inner if it == 0 else part(MID + 8 * other, 56)
+        land = part(PAD + 16 * other, HALF) if it == 0 else frame_rows
+        their_land = part(PAD + 16 * core, HALF) if it == 0 else part(MID + 8 * core, 56)
         back = []
         for n, (dy, dx) in enumerate(OFFSETS):
             q = far(dy, dx)
             back.append(
-                go(remote(sums.at[it, q], starts.at[it + 1, 0, chip, their_land], back_send.at[it, n], back_recv.at[it, n], (2 * q + other, sp)))
+                go(remote(sums.at[it, q, their_rows], starts.at[it + 1, 0, chip, their_land], back_send.at[it, n], back_recv.at[it, n], (2 * q + other, sp)))
             )
-        back.append(go(remote(sums.at[it, chip], starts.at[it + 1, 0, chip, their_land], back_send.at[it, 7], back_recv.at[it, 7], partner)))
-
+        back.append(go(remote(sums.at[it, chip, their_rows], starts.at[it + 1, 0, chip, their_land], back_send.at[it, 7], back_recv.at[it, 7], partner)))
+
+        for n, (dy, dx) in enumerate(OFFSETS):
+            @pl.when((source(dy, dx) < chip) | (source(dy, dx) == 7))
+            def _():
+                rim_copy(it, n).wait_recv()
+        rim_c = rim_gain[:, rim_out]
+        rim_c2 = rim_c * rim_c
+        total = rim_got[it, 7]
+        for k in range(7):
+            total = jnp.where(k < chip, rim_c2 * total + rim_got[it, k], total)
+        starts[it + 1, 0, :, rim_at] = total
+        starts[it + 1, 1, :, rim_at] = rim_c * total + rim_corr0[...]
         if it == 0:
-            for n, (dy, dx) in enumerate(OFFSETS):
-                @pl.when((source(dy, dx) < chip) | (source(dy, dx) == 7))
-                def _():
-                    rim_copy(n).wait_recv()
-            rim_c = rim_gain[:, rim_out]
-            rim_c2 = rim_c * rim_c
-            total = rim_got[7]
-            for k in range(7):
-                total = jnp.where(k < chip, rim_c2 * total + rim_got[k], total)
-            starts[1, 0, :, rim_at] = total
-            starts[1, 1, :, rim_at] = rim_c * total + rim_corr0[...]
             outer_halo = go(
-                remote(starts.at[1, :, :, rim_at], starts.at[1, :, :, part(PAD + 72 * other, 8)], halo_send, halo_recv, (pair + other, outer))
+                remote(starts.at[1, :, :, rim_at], rim.at[1, :, :, part(8 + 16 * other, 8)], halo_send, halo_recv, (pair + other, outer))
             )
+        else:
+            outs = [
+                go(remote(starts.at[2, other, :, rim_at], out_s.at[:, part(120 * core, 8)], outs_send.at[8], outs_recv.at[8], partner))
+            ]
+            out_s[:, part(120 * core, 8)] = starts[2, core, :, rim_at]
 
         def spread(t):
-            starts[it + 1, 1, t, land] = gain[it, t, inner] * starts[it + 1, 0, t, land] + corr0[it, t]
+            starts[it + 1, 1, t, land] = gain[it, t, frame_rows] * starts[it + 1, 0, t, land] + corr0[it, t, rows]
 
         if it == 0:
             for n in reversed(range(8)):
                 back[n].wait_recv()
                 spread(source(*OFFSETS[n]) if n < 7 else chip)
-            outer_halo.wait_recv()
         else:
-            outs = []
+            out_rows = part(HALF * core + 8 * other, 56)
             for n in reversed(range(8)):
                 back[n].wait_recv()
                 t = source(*OFFSETS[n]) if n < 7 else chip
                 spread(t)
                 outs.append(
-                    go(remote(starts.at[2, other, t, inner], out_s.at[t, own_half], outs_send.at[n], outs_recv.at[n], partner))
+                    go(remote(starts.at[2, other, t, land], out_s.at[t, out_rows], outs_send.at[n], outs_recv.at[n], partner))
                 )
-                out_s[t, own_half] = starts[2, core, t, inner]
-
+                out_s[t, out_rows] = starts[2, core, t, land]
+
+    for cp in edge_copies():
+        cp.wait_send()
     cp_e.wait_recv()
     for cp in outs:
         cp.wait_recv()
@@ -392,7 +445,8 @@
     for n, offset in enumerate(OFFSETS):
         @pl.when((far(*offset) > chip) | chip7)
         def _():
-            rim_copy(n).wait_send()
+            for it in range(2):
+                rim_copy(it, n).wait_send()
 
 
 def hand_out(s_ref, e_ref, starts_hbm, ends_hbm, buf, sem):
@@ -428,12 +482,12 @@
             vmem(1, 1024), vmem(1, 1024), ints(1024), vmem(8, 128), vmem(8, 128), ints(8, 128),
             vmem(3, 2, 8, ROWS), vmem(2, 2, 8, ROWS),
             vmem(2, 8, ROWS), vmem(2, 8, ROWS), vmem(2, 8, ROWS), vmem(2, 8, ROWS), vmem(2, HALF), vmem(10, ROWS), vmem(8, ROWS), vmem(10, ROWS),
-            ints(8, EDGE), vmem(2, 8, EDGE), vmem(2, 8, EDGE), vmem(8, EDGE), vmem(8, EDGE), vmem(8, EDGE), vmem(8, EDGE),
-            vmem(8, EDGE), vmem(8, EDGE), vmem(8, EDGE), vmem(2, 8, 8), vmem(8, 8), vmem(8, 8), vmem(8, 8, 8),
+            ints(8, EDGE), vmem(2, 2, 8, EDGE), vmem(2, 8, EDGE), vmem(8, EDGE), vmem(8, EDGE), vmem(8, EDGE), vmem(8, EDGE),
+            vmem(8, EDGE), vmem(8, EDGE), vmem(8, EDGE), vmem(2, 8, 8), vmem(8, 8), vmem(2, 8, 8), vmem(2, 8, 8, 8),
             vmem(2, 2, 8, HALF), vmem(2, 8, HALF), vmem(2, 8, HALF), vmem(2, 8, HALF), vmem(2, 8, HALF),
-            pltpu.SemaphoreType.REGULAR((2,)), sem(4, 4), sem(2), sem(2), sem(2, 2), sem(2, 2), one, one,
-            sem(2, 8), sem(2, 8), sem(2, 8), sem(2, 8), sem(7), sem(7), one, one,
-            one, one, sem(8), sem(8),
+            pltpu.SemaphoreType.REGULAR, sem(4, 4), sem(2), sem(2), sem(2, 2), sem(2, 2), one, one,
+            sem(2, 8), sem(2, 8), sem(2, 8), sem(2, 8), sem(2, 7), sem(2, 7), one, one,
+            one, one, sem(9), sem(9),
         ],
         compiler_params=pltpu.CompilerParams(
             collective_id=0, has_side_effects=True, vmem_limit_bytes=40 * 2**20

time: 42.6 us -> 41.7 us (0.979)
  the two profiles are of different devices: /device:TPU:1 before, /device:TPU:33 now
where the time goes in v6:
time: 41.7 us; the launch traced here: 41.6 us
  Pallas kernels  41 us (98%)
  between operations  0.64 us (2%)
    pallas_call x1, Pallas kernels, local(): pl.pallas_call(kernel, out_shape=(held, held), in_specs=[hbm] * 6, out_sp...  39.8 us
    pallas_call x1, Pallas kernels, local(): pl.pallas_call(hand_out, out_shape=(block, block), in_specs=[in_vmem] * 2...  1.19 us

profile of v6, /device:TPU:33, one launch (start us, length us, event | category | flops | bytes accessed | tf_op | source)
XLA Modules:
  0.0 41.6 jit_solution(10366840893620647575)
XLA Ops:
  0.6 39.8 %parareal.1 = (f32[8,128,128]{2,1,0:T(8,128)S(1)}, f32[8,128,128]{2,1,0:T(8,128)S(1)}) custom-call(f32[8]{0:T(128)} %base_hbm.1, f32[8]{0:T(128)} %satur_hbm.1, f32[8]{0:T(128)} %mob_hbm.1, f32[1,1024,128]{2,1,0:T(8,128)} %a_hbm.1, f32[1,1024,128]{2,1,0:T(8,128)} %j_hbm.1, s32[1024,128]{1,0:T(8,128)} %r_hbm.1), custom_call_target="tpu_custom_call" | custom-call | tf_op jit(solution)/shard_map/parareal/pallas_call | solution.py:475
  40.4 1.2 %hand_out.1 = (f32[1,1024,128]{2,1,0:T(8,128)}, f32[1,1024,128]{2,1,0:T(8,128)}) custom-call(f32[8,128,128]{2,1,0:T(8,128)S(1)} %get-tuple-element.4.s_ref, f32[8,128,128]{2,1,0:T(8,128)S(1)} %get-tuple-element.5.e_ref), custom_call_target="tpu_custom_call" | custom-call | tf_op jit(solution)/shard_map/hand_out/pallas_call | solution.py:497

commit v7 on v6

--- a/solution.py
+++ b/solution.py
@@ -102,8 +102,20 @@
     barrier = pltpu.get_barrier_semaphore()
     tellers = [(2 * far(1, 0) + core, sp), (2 * far(1, 0) + other, sp), partner]
     near = [(2 * far(0, dx) + core, sp) for dx in (1, 3, 2)] + tellers
-    for device in near:
-        pl.semaphore_signal(barrier, inc=1, device_id=device, device_id_type=MESH)
+    plane = lax.rem(sp, 8)
+    is_first, is_last = plane == 0, plane == 7
+    edge_sources = [(pair, outer), (pair + 1, outer)]
+
+    def greet(devices):
+        for device in devices:
+            pl.semaphore_signal(barrier, inc=1, device_id=device, device_id_type=MESH)
+
+    greet(near)
+    later_greeting = (is_first & (core == 0)) | (is_last & (core == 1))
+
+    @pl.when(jnp.logical_not(later_greeting))
+    def _():
+        greet(edge_sources)
 
     loads = []
     for n, (src, dst, pieces) in enumerate(((a_hbm.at[0], in_a.at[0], 4), (j_hbm.at[0], in_j.at[0], 4), (r_hbm, in_r, 4))):
@@ -194,46 +206,52 @@
     starts[0, core, :, wide] = ta[:, mine]
     drive[0, core, :, wide] = tj[:, mine]
 
-    even = lax.rem(sp, 2) == 0
-    edge_sources = [(pair, outer), (pair + 1, outer)]
-
-    def greet(devices):
-        for device in devices:
-            pl.semaphore_signal(barrier, inc=1, device_id=device, device_id_type=MESH)
-
-    @pl.when(even)
+    @pl.when(is_first)
     def _():
-        pl.semaphore_wait(barrier, len(near))
-        greet(edge_sources + [(tm, jnp.where(core == 0, right, left))])
-
-    @pl.when(jnp.logical_not(even))
+        pl.semaphore_wait(barrier, len(near) + 1)
+        greet([(pair + 1, left)])
+
+        @pl.when(core == 0)
+        def _():
+            greet([(pair, left)])
+
+    @pl.when(is_last & (core == 1))
     def _():
         pl.semaphore_wait(barrier, len(near) + 3)
         greet(edge_sources)
 
+    @pl.when(jnp.logical_not(is_first | (is_last & (core == 1))))
+    def _():
+        pl.semaphore_wait(barrier, len(near) + 2)
+
     for device in tellers:
         pl.semaphore_signal(word, inc=1, device_id=device, device_id_type=MESH)
 
-    def edge_copies():
-        copies = []
-        for n, (src, dst) in enumerate(((ta, rim.at[0]), (tj, rim_drive))):
-            copies.append(
-                remote(src.at[:, pl.ds(120, 8)], dst.at[core, :, pl.ds(8, 8)], edge_send.at[n, 0], edge_recv.at[n, core], (pair, right))
-            )
-            copies.append(
-                remote(src.at[:, pl.ds(0, 8)], dst.at[core, :, pl.ds(24, 8)], edge_send.at[n, 1], edge_recv.at[n, core], (pair + 1, left))
-            )
+    def right_edge(n, src, dst):
+        return remote(src.at[:, pl.ds(120, 8)], dst.at[core, :, pl.ds(8, 8)], edge_send.at[n, 0], edge_recv.at[n, core], (pair, right))
+
+    def left_edge(n, src, dst):
+        return remote(src.at[:, pl.ds(0, 8)], dst.at[core, :, pl.ds(24, 8)], edge_send.at[n, 1], edge_recv.at[n, core], (pair + 1, left))
+
+    def region_edge():
         ahead = (tm, jnp.where(core == 0, right, left))
-        copies.append(remote(tr.at[:, part(120 * other, 8)], rim_r.at[:, rim_halo], reg_send, reg_recv, ahead))
-        return copies
+        return remote(tr.at[:, part(120 * other, 8)], rim_r.at[:, rim_halo], reg_send, reg_recv, ahead)
+
+    edges = ((0, ta, rim.at[0]), (1, tj, rim_drive))
 
     def send_pair(n, src, dst):
         return go(remote(src.at[:, theirs], dst.at[core, :, wide], pair_send.at[n], pair_recv.at[n], partner))
 
-    @pl.when(jnp.logical_not(even))
+    for edge in edges:
+        right_edge(*edge).start()
+
+        @pl.when(jnp.logical_not(is_first))
+        def _():
+            left_edge(*edge).start()
+
+    @pl.when(jnp.logical_not(is_first & (core == 1)))
     def _():
-        for cp in edge_copies():
-            cp.start()
+        region_edge().start()
 
     pairs = [send_pair(0, ta, starts.at[0]), send_pair(1, tj, drive.at[0])]
 
@@ -313,13 +331,17 @@
         there.append(go(remote(mine_out, land, there_send.at[it, 7], there_recv.at[it, 7], partner)))
 
         if it == 0:
-            @pl.when(even)
+            @pl.when(is_first)
             def _():
-                pl.semaphore_wait(barrier, 2)
-                for cp in edge_copies():
-                    cp.start()
-
-            edge_copies()[-1].wait_recv()
+                pl.semaphore_wait(barrier, 1)
+                for edge in edges:
+                    left_edge(*edge).start()
+
+                @pl.when(core == 1)
+                def _():
+                    region_edge().start()
+
+            region_edge().wait_recv()
             look_up(rim_r, 8 + 16 * core, 8, put_rim)
             for ref, into in zip(coefs, rim_coefs):
                 into[:, rim_own] = ref[0, :, rim_from]
@@ -435,8 +457,10 @@
                 )
                 out_s[t, out_rows] = starts[2, core, t, land]
 
-    for cp in edge_copies():
-        cp.wait_send()
+    for edge in edges:
+        right_edge(*edge).wait_send()
+        left_edge(*edge).wait_send()
+    region_edge().wait_send()
     cp_e.wait_recv()
     for cp in outs:
         cp.wait_recv()

time: 41.7 us -> 39.7 us (0.952)
  the two profiles are of different devices: /device:TPU:33 before, /device:TPU:1 now
where the time goes in v7:
time: 39.7 us; the launch traced here: 39.3 us
  Pallas kernels  38.7 us (97%)
  between operations  0.64 us (2%)
    pallas_call x1, Pallas kernels, local(): pl.pallas_call(kernel, out_shape=(held, held), in_specs=[hbm] * 6, out_sp...  37.5 us
    pallas_call x1, Pallas kernels, local(): pl.pallas_call(hand_out, out_shape=(block, block), in_specs=[in_vmem] * 2...  1.19 us

profile of v7, /device:TPU:1, one launch (start us, length us, event | category | flops | bytes accessed | tf_op | source)
XLA Modules:
  0.0 39.3 jit_solution(9640465918378405712)
XLA Ops:
  0.6 37.5 %parareal.1 = (f32[8,128,128]{2,1,0:T(8,128)S(1)}, f32[8,128,128]{2,1,0:T(8,128)S(1)}) custom-call(f32[8]{0:T(128)} %base_hbm.1, f32[8]{0:T(128)} %satur_hbm.1, f32[8]{0:T(128)} %mob_hbm.1, f32[1,1024,128]{2,1,0:T(8,128)} %a_hbm.1, f32[1,1024,128]{2,1,0:T(8,128)} %j_hbm.1, s32[1024,128]{1,0:T(8,128)} %r_hbm.1), custom_call_target="tpu_custom_call" | custom-call | tf_op jit(solution)/shard_map/parareal/pallas_call | solution.py:499
  38.1 1.2 %hand_out.1 = (f32[1,1024,128]{2,1,0:T(8,128)}, f32[1,1024,128]{2,1,0:T(8,128)}) custom-call(f32[8,128,128]{2,1,0:T(8,128)S(1)} %get-tuple-element.4.s_ref, f32[8,128,128]{2,1,0:T(8,128)S(1)} %get-tuple-element.5.e_ref), custom_call_target="tpu_custom_call" | custom-call | tf_op jit(solution)/shard_map/hand_out/pallas_call | solution.py:521

commit v8 on v7

--- a/solution.py
+++ b/solution.py
@@ -13,7 +13,7 @@
 ROWS = 96
 EDGE = 40
 F32 = jnp.float32
-OFFSETS = ((1, 2), (1, 1), (1, 3), (0, 2), (1, 0), (0, 1), (0, 3))
+OFFSETS = ((1, 2), (1, 1), (0, 2), (1, 3), (0, 1), (1, 0), (0, 3))
 
 
 def part(start, size):

time: 39.7 us -> 39.6 us (level)
  no operation moved by 1% of the time
where the time goes in v8:
time: 39.6 us; the launch traced here: 39.5 us
  Pallas kernels  38.9 us (98%)
  between operations  0.64 us (2%)
    pallas_call x1, Pallas kernels, local(): pl.pallas_call(kernel, out_shape=(held, held), in_specs=[hbm] * 6, out_sp...  37.7 us
    pallas_call x1, Pallas kernels, local(): pl.pallas_call(hand_out, out_shape=(block, block), in_specs=[in_vmem] * 2...  1.19 us

profile of v8, /device:TPU:1, one launch (start us, length us, event | category | flops | bytes accessed | tf_op | source)
XLA Modules:
  0.0 39.5 jit_solution(17140235032783442336)
XLA Ops:
  0.6 37.7 %parareal.1 = (f32[8,128,128]{2,1,0:T(8,128)S(1)}, f32[8,128,128]{2,1,0:T(8,128)S(1)}) custom-call(f32[8]{0:T(128)} %base_hbm.1, f32[8]{0:T(128)} %satur_hbm.1, f32[8]{0:T(128)} %mob_hbm.1, f32[1,1024,128]{2,1,0:T(8,128)} %a_hbm.1, f32[1,1024,128]{2,1,0:T(8,128)} %j_hbm.1, s32[1024,128]{1,0:T(8,128)} %r_hbm.1), custom_call_target="tpu_custom_call" | custom-call | tf_op jit(solution)/shard_map/parareal/pallas_call | solution.py:499
  38.3 1.2 %hand_out.1 = (f32[1,1024,128]{2,1,0:T(8,128)}, f32[1,1024,128]{2,1,0:T(8,128)}) custom-call(f32[8,128,128]{2,1,0:T(8,128)S(1)} %get-tuple-element.4.s_ref, f32[8,128,128]{2,1,0:T(8,128)S(1)} %get-tuple-element.5.e_ref), custom_call_target="tpu_custom_call" | custom-call | tf_op jit(solution)/shard_map/hand_out/pallas_call | solution.py:521

commit v9 on v8

--- a/solution.py
+++ b/solution.py
@@ -118,7 +118,7 @@
         greet(edge_sources)
 
     loads = []
-    for n, (src, dst, pieces) in enumerate(((a_hbm.at[0], in_a.at[0], 4), (j_hbm.at[0], in_j.at[0], 4), (r_hbm, in_r, 4))):
+    for n, (src, dst, pieces) in enumerate(((a_hbm.at[0], in_a.at[0], 2), (j_hbm.at[0], in_j.at[0], 1), (r_hbm, in_r, 1))):
         size = 1024 // pieces
         loads.append([])
         for k in range(pieces):
@@ -242,6 +242,8 @@
     def send_pair(n, src, dst):
         return go(remote(src.at[:, theirs], dst.at[core, :, wide], pair_send.at[n], pair_recv.at[n], partner))
 
+    pairs = [send_pair(0, ta, starts.at[0]), send_pair(1, tj, drive.at[0])]
+
     for edge in edges:
         right_edge(*edge).start()
 
@@ -252,8 +254,6 @@
     @pl.when(jnp.logical_not(is_first & (core == 1)))
     def _():
         region_edge().start()
-
-    pairs = [send_pair(0, ta, starts.at[0]), send_pair(1, tj, drive.at[0])]
 
     chip7 = chip == 7
 

time: 39.6 us -> 40.7 us (1.028)
  Pallas kernels: 38.9 us -> 39.9 us
    pallas_call x1, Pallas kernels: 37.7 us -> 38.7 us  [local(): pl.pallas_call(kernel, out_shape=(held, held), in_specs=[hbm] * 6, out_sp...]
where the time goes in v9:
time: 40.7 us; the launch traced here: 40.6 us
  Pallas kernels  39.9 us (98%)
  between operations  0.64 us (2%)
    pallas_call x1, Pallas kernels, local(): pl.pallas_call(kernel, out_shape=(held, held), in_specs=[hbm] * 6, out_sp...  38.7 us
    pallas_call x1, Pallas kernels, local(): pl.pallas_call(hand_out, out_shape=(block, block), in_specs=[in_vmem] * 2...  1.19 us

profile of v9, /device:TPU:1, one launch (start us, length us, event | category | flops | bytes accessed | tf_op | source)
XLA Modules:
  0.0 40.6 jit_solution(140952601247514979)
XLA Ops:
  0.6 38.7 %parareal.1 = (f32[8,128,128]{2,1,0:T(8,128)S(1)}, f32[8,128,128]{2,1,0:T(8,128)S(1)}) custom-call(f32[8]{0:T(128)} %base_hbm.1, f32[8]{0:T(128)} %satur_hbm.1, f32[8]{0:T(128)} %mob_hbm.1, f32[1,1024,128]{2,1,0:T(8,128)} %a_hbm.1, f32[1,1024,128]{2,1,0:T(8,128)} %j_hbm.1, s32[1024,128]{1,0:T(8,128)} %r_hbm.1), custom_call_target="tpu_custom_call" | custom-call | tf_op jit(solution)/shard_map/parareal/pallas_call | solution.py:499
  39.4 1.2 %hand_out.1 = (f32[1,1024,128]{2,1,0:T(8,128)}, f32[1,1024,128]{2,1,0:T(8,128)}) custom-call(f32[8,128,128]{2,1,0:T(8,128)S(1)} %get-tuple-element.4.s_ref, f32[8,128,128]{2,1,0:T(8,128)S(1)} %get-tuple-element.5.e_ref), custom_call_target="tpu_custom_call" | custom-call | tf_op jit(solution)/shard_map/hand_out/pallas_call | solution.py:521
